TPU v7x, 512 devices: a whole 4x8x8 slice. The times are simulated.
512 devices in a mesh: gx: 32 (over y, x_hi, core), gy: 16 (over x_lo, z).
Axes of the slice: x: 4 (x_hi: 2, x_lo: 2; x = x_hi * 2 + x_lo), y: 8, z: 8, core: 2. Of those that a mesh axis runs over, the one named last changes fastest.
Arguments:
- fine_now: float32 [3, 384, 192, 128], P(None, 'gx', 'gy'), may hold values from -6 to 6
- fine_prev: float32 [3, 384, 192, 128], P(None, 'gx', 'gy'), may hold values from -6 to 6
- fine_mu: float32 [384, 192, 128], P('gx', 'gy'), may hold values from 0.5 to 2
- fine_coef: float32 [384, 192, 128], P('gx', 'gy'), may hold values from 0.03 to 0.12
- coarse_now: float32 [3, 192, 96, 128], P(None, 'gx', 'gy'), may hold values from -6 to 6
- coarse_prev: float32 [3, 192, 96, 128], P(None, 'gx', 'gy'), may hold values from -6 to 6
- coarse_mu: float32 [192, 96, 128], P('gx', 'gy'), may hold values from 0.5 to 2
- coarse_coef: float32 [192, 96, 128], P('gx', 'gy'), may hold values from 0.03 to 0.12
- src_cell: int32 [3, 4096], replicated, may hold values from 0 to 383, as said below
- src_moment: float32 [6, 4096], P(None, ('gx', 'gy')), may hold values from -48 to 48
Outputs:
- fine_next: float32 [3, 384, 192, 128], P(None, 'gx', 'gy')
- coarse_next: float32 [3, 192, 96, 128], P(None, 'gx', 'gy')
- ghost: float32 [3, 192, 96], P(None, 'gx', 'gy')
Inputs may be any that keep to these rules, and one draw needn't show every extreme that they name: `src_cell`: row 0 holds x indices below 384, row 1 y indices below 192, row 2 depth indices below 128.
All inputs are finite; a program needn't handle non-finite values.
Results may differ from a plain program's by a relative error of at most 0.00013.
Values sent between devices are 32-bit elements; how exact they have to be, the bound alone decides.
No kernel may reach another device: no remote copies, remote signals or barrier semaphores. Data moves between devices by JAX's collectives and lax.ppermute only.
A program may use at most 64 MiB of HBM per device.

v0:
```python
import jax
import jax.numpy as jnp
from jax import lax
from jax.sharding import PartitionSpec as P

ITERS = 3


def with_halo(x, sides, width):
    for axis, dim in sides:
        size, length = (lax.axis_size(axis), x.shape[dim])
        up = [(i, (i + 1) % size) for i in range(size - 1)]
        down = [(j, i) for i, j in up]
        last = lax.slice_in_dim(x, length - width, length, axis=dim)
        initial = lax.slice_in_dim(x, 0, width, axis=dim)
        before = lax.ppermute(last, axis, up)
        after = lax.ppermute(initial, axis, down)
        x = jnp.concatenate([before, x, after], axis=dim)
    return x


def prolong_table(count):
    coarse_index = lax.broadcasted_iota(jnp.int32, (count, 2 * count - 1), 0)
    fine_index = lax.broadcasted_iota(jnp.int32, (count, 2 * count - 1), 1)
    exact = fine_index == 2 * coarse_index
    halfway = (fine_index == 2 * coarse_index + 1) | (fine_index == 2 * coarse_index - 1)
    return jnp.where(exact, 1.0, jnp.where(halfway, 0.5, 0.0)).astype(jnp.float32)


def restrict_table(finer_count):
    count = (finer_count - 1) // 2
    fine_index = lax.broadcasted_iota(jnp.int32, (finer_count, count), 0)
    coarse_index = lax.broadcasted_iota(jnp.int32, (finer_count, count), 1)
    outer = (fine_index == 2 * coarse_index) | (fine_index == 2 * coarse_index + 2)
    centre = fine_index == 2 * coarse_index + 1
    return jnp.where(centre, 0.5, jnp.where(outer, 0.25, 0.0)).astype(jnp.float32)


def prolong_plane(coarse):
    along_y = jnp.einsum(
        "cxy,yb->cxb", coarse, prolong_table(coarse.shape[2]), precision=lax.Precision.HIGHEST
    )
    return jnp.einsum(
        "cxb,xa->cab", along_y, prolong_table(coarse.shape[1]), precision=lax.Precision.HIGHEST
    )


def restrict_plane(finer):
    along_y = jnp.einsum(
        "cxy,yb->cxb", finer, restrict_table(finer.shape[2]), precision=lax.Precision.HIGHEST
    )
    return jnp.einsum(
        "cxb,xa->cab", along_y, restrict_table(finer.shape[1]), precision=lax.Precision.HIGHEST
    )


def coupled_terms(ghost_wide):
    finer = prolong_plane(ghost_wide)
    return restrict_plane(finer[:, 1:, 1:])


def horizontal_terms(wide):
    size_x = wide.shape[1] - 4
    size_y = wide.shape[2] - 4
    rows = wide[:, :, 2 : 2 + size_y]
    along_x = (
        -rows[:, 0:size_x]
        + 16.0 * rows[:, 1 : size_x + 1]
        - 30.0 * rows[:, 2 : size_x + 2]
        + 16.0 * rows[:, 3 : size_x + 3]
        - rows[:, 4 : size_x + 4]
    ) / 12.0
    cols = wide[:, 2 : 2 + size_x]
    along_y = (
        -cols[:, :, 0:size_y]
        + 16.0 * cols[:, :, 1 : size_y + 1]
        - 30.0 * cols[:, :, 2 : size_y + 2]
        + 16.0 * cols[:, :, 3 : size_y + 3]
        - cols[:, :, 4 : size_y + 4]
    ) / 12.0
    return along_x + along_y


def vertical_terms(field, upper, lower):
    above = jnp.concatenate([upper[..., None], field[..., :-1]], axis=-1)
    below = jnp.concatenate([field[..., 1:], lower[..., None]], axis=-1)
    return above - 2.0 * field + below


def source_force(cells, moments, start_x, start_y, size_x, size_y, size_z):
    pairs = (
        (0, 0, 0),
        (0, 1, 3),
        (0, 2, 4),
        (1, 0, 3),
        (1, 1, 1),
        (1, 2, 5),
        (2, 0, 4),
        (2, 1, 5),
        (2, 2, 2),
    )
    limits = (size_x, size_y, size_z)
    comp_list = []
    place_lists = ([], [], [])
    value_list = []
    for component, direction, moment_row in pairs:
        for sign_value in (1, -1):
            shifted = [cells[0] - start_x, cells[1] - start_y, cells[2]]
            shifted[direction] = shifted[direction] + sign_value
            inside = jnp.ones(cells.shape[1:], bool)
            for axis_number in range(3):
                inside = (
                    inside
                    & (shifted[axis_number] >= 0)
                    & (shifted[axis_number] < limits[axis_number])
                )
            for axis_number in range(3):
                place_lists[axis_number].append(
                    jnp.where(inside, shifted[axis_number], limits[axis_number])
                )
            comp_list.append(jnp.full(cells.shape[1:], component, jnp.int32))
            value_list.append(sign_value * 0.5 * moments[moment_row])
    force = jnp.zeros((3, size_x, size_y, size_z), moments.dtype)
    return force.at[
        jnp.concatenate(comp_list),
        jnp.concatenate(place_lists[0]),
        jnp.concatenate(place_lists[1]),
        jnp.concatenate(place_lists[2]),
    ].add(jnp.concatenate(value_list), mode="drop")


def neighbour_rim(ghost):
    return with_halo(ghost, (("gx", 1), ("gy", 2)), 1)


def local(
    fine_now,
    fine_prev,
    fine_mu,
    fine_coef,
    coarse_now,
    coarse_prev,
    coarse_mu,
    coarse_coef,
    src_cell,
    src_moment,
):
    fine_x = fine_now.shape[1]
    fine_y = fine_now.shape[2]
    depth = fine_now.shape[3]
    coarse_x = coarse_now.shape[1]
    coarse_y = coarse_now.shape[2]
    fine_wide, coarse_wide = (
        with_halo(fine_now, (("gx", 1), ("gy", 2)), 2),
        with_halo(coarse_now, (("gx", 1), ("gy", 2)), 2),
    )
    inverse_diag = 1.0 / (0.6 + coarse_mu[:, :, 0])
    lower_plane = fine_wide[:, 1 : fine_x + 3, 1 : fine_y + 3, depth - 2]
    forcing = restrict_plane(lower_plane) + 2.0 * coarse_now[..., 0] - coarse_now[..., 1]
    ghost = inverse_diag * forcing
    for sweep_index in range(ITERS):
        ghost = inverse_diag * (forcing + coupled_terms(neighbour_rim(ghost)))
    ghost_wide = neighbour_rim(ghost)
    fine_ghost = prolong_plane(ghost_wide)[:, 2 : 2 + fine_x, 2 : 2 + fine_y]
    ghost_own = ghost_wide[:, 1 : 1 + coarse_x, 1 : 1 + coarse_y]
    moments_all = lax.all_gather(src_moment, ("gx", "gy"), axis=1, tiled=True)
    start_x = lax.axis_index("gx") * fine_x
    start_y = lax.axis_index("gy") * fine_y
    force = source_force(src_cell, moments_all, start_x, start_y, fine_x, fine_y, depth)
    fine_terms = horizontal_terms(fine_wide) + vertical_terms(
        fine_now, fine_now[..., 1], fine_ghost
    )
    fine_next = 2.0 * fine_now - fine_prev + fine_coef[None] * (fine_mu[None] * fine_terms + force)
    coarse_terms = horizontal_terms(coarse_wide) + vertical_terms(
        coarse_now, ghost_own, jnp.zeros_like(ghost_own)
    )
    coarse_next = (
        2.0 * coarse_now - coarse_prev + coarse_coef[None] * (coarse_mu[None] * coarse_terms * 0.25)
    )
    return (fine_next, coarse_next, ghost_own)


def solution(mesh):
    in_specs = (
        P(None, "gx", "gy", None),
        P(None, "gx", "gy", None),
        P("gx", "gy", None),
        P("gx", "gy", None),
        P(None, "gx", "gy", None),
        P(None, "gx", "gy", None),
        P("gx", "gy", None),
        P("gx", "gy", None),
        P(),
        P(None, ("gx", "gy")),
    )
    out_specs = (P(None, "gx", "gy", None), P(None, "gx", "gy", None), P(None, "gx", "gy"))
    return jax.shard_map(local, mesh=mesh, in_specs=in_specs, out_specs=out_specs, check_vma=False)
```

profile of v0, /device:TPU:34, one launch (start us, length us, event | category | flops | bytes accessed | tf_op | source)
XLA Modules:
  0.0 1788.9 jit_solution(2442975527248595487)
XLA Ops:
  3.4 7.3 collective-permute-start.1
  13.4 7.3 collective-permute-start.21
  30.1 1240.9 %all_gather.3 = f32[6,4096]{0,1:T(8,128)S(1)} all-gather(f32[6,8]{0,1:T(8,128)S(1)} %copy.197), channel_id=1, replica_groups=mesh['gx'=32,'gy'=16] {'gx','gy'}, dimensions={1}, use_global_device_ids=true | all-gather | bytes 98496 | tf_op jit(solution)/shard_map/all_gather | solution.py:166
  1271.0 9.4 multiply_reduce_fusion
  1284.3 3.9 collective-permute-start.2
  1288.3 6.5 collective-permute-start.23
  1299.7 2.4 collective-permute-start.4
  1302.1 6.1 collective-permute-done.4
  1308.3 6.0 collective-permute-start.7
  1316.3 5.8 collective-permute-done.6
  1325.2 2.4 collective-permute-start.8
  1327.6 6.1 collective-permute-done.8
  1336.0 3.6 collective-permute-start.10
  1339.6 4.5 collective-permute-done.10
  1347.3 2.4 collective-permute-start.12
  1349.7 6.1 collective-permute-done.12
  1355.9 5.1 collective-permute-start.15
  1362.9 5.8 collective-permute-done.14
  1371.8 2.4 collective-permute-start.16
  1375.3 5.1 collective-permute-done.16
  1380.4 3.1 collective-permute-start.19
  1383.6 2.7 collective-permute-start.18
  1386.3 5.0 collective-permute-done.18
  1395.1 393.0 %scatter_fusion = f32[55296]{0:T(1024)S(1)} fusion(f32[55296]{0:T(1024)S(1)} %reshape.2847, s32[73728]{0:T(1024)S(1)} %broadcast_select_fusion, f32[73728]{0:T(1024)} %copy-done.3), kind=kCustom, calls=%fused_computation | custom fusion | flops 73728 | bytes 1179648
  (212 shorter events, 44.3 us)
Async XLA Ops:
  1.5 1280.6 %collective-permute-start = (f32[3,2,12,128]{3,2,1,0:T(8,128)S(1)}, f32[3,2,12,128]{3,2,1,0:T(8,128)S(1)}, u32[]{:S(2)}, u32[]{:S(2)}) collective-permute-start(f32[3,2,12,128]{3,2,1,0:T(8,128)S(1)} %get-tuple-element.52), channel_id=1, source_target_pairs={{0,16},{16,32},{32,48},{48,64},{64,80},{80,96},{96,112},{112,128},... | collective-permute-start | bytes 110600 | tf_op jit(solution)/shard_map/ppermute | solution.py:16
  3.4 1278.8 %collective-permute-start.1 = (f32[3,2,12,128]{3,2,1,0:T(8,128)S(1)}, f32[3,2,12,128]{3,2,1,0:T(8,128)S(1)}, u32[]{:S(2)}, u32[]{:S(2)}) collective-permute-start(f32[3,2,12,128]{3,2,1,0:T(8,128)S(1)} %get-tuple-element.51), channel_id=1, source_target_pairs={{16,0},{32,16},{48,32},{64,48},{80,64},{96,80},{112,96},{128,112},... | collective-permute-start | bytes 110600 | tf_op jit(solution)/shard_map/ppermute | solution.py:17
  11.5 1270.6 %collective-permute-start.20 = (f32[3,2,6,128]{3,2,1,0:T(8,128)S(1)}, f32[3,2,6,128]{3,2,1,0:T(8,128)S(1)}, u32[]{:S(2)}, u32[]{:S(2)}) collective-permute-start(f32[3,2,6,128]{3,2,1,0:T(8,128)S(1)} %get-tuple-element.61), channel_id=1, source_target_pairs={{0,16},{16,32},{32,48},{48,64},{64,80},{80,96},{96,112},{112,128},... | collective-permute-start | bytes 55304 | tf_op jit(solution)/shard_map/ppermute | solution.py:16
  13.4 1268.7 %collective-permute-start.21 = (f32[3,2,6,128]{3,2,1,0:T(8,128)S(1)}, f32[3,2,6,128]{3,2,1,0:T(8,128)S(1)}, u32[]{:S(2)}, u32[]{:S(2)}) collective-permute-start(f32[3,2,6,128]{3,2,1,0:T(8,128)S(1)} %get-tuple-element.60), channel_id=1, source_target_pairs={{16,0},{32,16},{48,32},{64,48},{80,64},{96,80},{112,96},{128,112},... | collective-permute-start | bytes 55304 | tf_op jit(solution)/shard_map/ppermute | solution.py:17
  1282.3 14.3 collective-permute-start.3
  1284.3 12.4 collective-permute-start.2
  1288.3 86.2 %collective-permute-start.23 = (f32[3,10,2,128]{3,2,1,0:T(2,128)S(1)}, f32[3,10,2,128]{3,2,1,0:T(2,128)S(1)}, u32[]{:S(2)}, u32[]{:S(2)}) collective-permute-start(f32[3,10,2,128]{3,2,1,0:T(2,128)S(1)} %get-tuple-element.54), channel_id=1, source_target_pairs={{1,0},{2,1},{3,2},{4,3},{5,4},{6,5},{7,6},{8,7},{9,8},{10,9},{11,1... | collective-permute-start | bytes 92168 | tf_op jit(solution)/shard_map/ppermute | solution.py:17
  1294.7 79.7 %collective-permute-start.22 = (f32[3,10,2,128]{3,2,1,0:T(2,128)S(1)}, f32[3,10,2,128]{3,2,1,0:T(2,128)S(1)}, u32[]{:S(2)}, u32[]{:S(2)}) collective-permute-start(f32[3,10,2,128]{3,2,1,0:T(2,128)S(1)} %get-tuple-element.53), channel_id=1, source_target_pairs={{0,1},{1,2},{2,3},{3,4},{4,5},{5,6},{6,7},{7,8},{8,9},{9,10},{10,1... | collective-permute-start | bytes 92168 | tf_op jit(solution)/shard_map/ppermute | solution.py:16
  1297.8 4.3 collective-permute-start.5
  1299.7 8.5 collective-permute-start.4
  1308.3 8.0 collective-permute-start.7
  1314.3 7.7 collective-permute-start.6
  1323.2 4.3 collective-permute-start.9
  1325.2 8.5 collective-permute-start.8
  1333.8 5.9 collective-permute-start.11
  1336.0 8.1 collective-permute-start.10
  1345.3 4.3 collective-permute-start.13
  1347.3 8.5 collective-permute-start.12
  1355.9 7.1 collective-permute-start.15
  1361.0 7.7 collective-permute-start.14
  1369.9 5.4 collective-permute-start.17
  1371.8 8.5 collective-permute-start.16
  1380.4 5.9 collective-permute-start.19
  1383.6 7.7 collective-permute-start.18
  (16 other events, 2807.2 us)
where the time goes:
time: 1790 us
  blocking collectives  1240 us (69%)
  other arithmetic  411 us (23%)
  starting transfers between devices  76.5 us (4%)
  waiting for transfers between devices  44.4 us (2%)
    all_gather x1, blocking collectives, local(): moments_all = lax.all_gather(src_moment, ('gx', 'gy'), axis=1, tiled=True)  1240 us
    unnamed x4, other arithmetic  396 us
    ppermute x12, starting transfers between devices, with_halo(): after = lax.ppermute(initial, axis, down)  47.1 us
    ppermute x12, waiting for transfers between devices, with_halo(): before = lax.ppermute(last, axis, up)  44.4 us
  transfers between devices with their start and end apart: 24, of which 8 were waited for; matrix products, arithmetic and copies ran while one was open for 1% of the time, Pallas kernels for 0%

commit v1 on v0

v1 whole, which is shorter than its diff:
```python
import functools

import jax
import jax.numpy as jnp
import numpy as np
from jax import lax
from jax.experimental import pallas as pl
from jax.experimental.pallas import tpu as pltpu
from jax.sharding import PartitionSpec as P

ITERS = 3
AX = ("gx", "gy")
ROWS = 128
GROW = 108
VMEM = pltpu.VMEM
SMEM = pltpu.SMEM
F32 = jnp.float32


def vspec(n):
    return [pl.BlockSpec(memory_space=VMEM)] * n


def lane_iota(shape):
    return lax.broadcasted_iota(jnp.int32, shape, len(shape) - 1)


def row_iota(shape):
    return lax.broadcasted_iota(jnp.int32, shape, 0)


def pack_x_kernel(fine, coarse, mu, mom, half, xu, xd, own, row_out, a_s, g_s):
    lane = lane_iota((1, 128))
    acc = jnp.zeros((12, 128), F32)
    for c in range(3):
        for x in range(12):
            at = c * 16 + 3 + x // 2
            if x % 2 == 0:
                w = jnp.where(lane == at, 0.5, 0.0)
            else:
                w = jnp.where((lane == at) | (lane == at + 1), 0.25, 0.0)
            acc = acc + fine[c, x, :, 126:127] * w
    a_s[...] = jnp.zeros((24, 128), F32)
    a_s[1:13, :] = acc
    g_s[...] = jnp.zeros((16, 128), F32)
    for j in range(7):
        g_s[3 + j : 4 + j, :] = (
            0.25 * a_s[2 * j : 2 * j + 1, :]
            + 0.5 * a_s[2 * j + 1 : 2 * j + 2, :]
            + 0.25 * a_s[2 * j + 2 : 2 * j + 3, :]
        )
    b = jnp.zeros((6, 128), F32)
    for i in range(6):
        for c in range(3):
            col = 2.0 * coarse[c, i, :, 0:1] - coarse[c, i, :, 1:2]
            b = b + jnp.where(lane == c * 16 + 3 + i, col, 0.0)
        inv = 1.0 / (0.6 + mu[i, :, 0:1])
        b = b + jnp.where(lane == 48 + 3 + i, inv, 0.0)
    g_s[3:9, :] = g_s[3:9, :] + b
    g = g_s[...]
    own[...] = g
    place = lane_iota((16, 128)) % 16
    for c in range(3):
        for j in range(2):
            at = 18 * (2 * c + j)
            xu[at : at + 12, :] = fine[c, 10 + j]
            xu[at + 12 : at + 18, :] = coarse[c, 4 + j]
            xd[at : at + 12, :] = fine[c, j]
            xd[at + 12 : at + 18, :] = coarse[c, j]
    xu[GROW : GROW + 16, :] = jnp.where(place < 4, pltpu.roll(g, 128 - 6, 1), 0.0)
    xd[GROW : GROW + 16, :] = jnp.where(
        (place >= 9) & (place < 13), pltpu.roll(g, 6, 1), 0.0
    )
    for ref in (xu, xd):
        ref[GROW + 16 : ROWS, :] = jnp.zeros((ROWS - GROW - 16, 128), F32)
    lanes = lane_iota((6, 128))
    want = 8 * row_iota((6, 128)) + 64 * half[0]
    t = jnp.zeros((6, 128), F32)
    for j in range(8):
        t = t + jnp.where(lanes == want + j, mom[:, j : j + 1], 0.0)
    row_out[...] = jnp.broadcast_to(jnp.sum(t, axis=0, keepdims=True), row_out.shape)


def pack_y_kernel(fine, coarse, own, rxu, rxd, yu, yd, gx):
    g = own[...] + rxu[GROW : GROW + 16, :] + rxd[GROW : GROW + 16, :]
    gx[...] = g
    for c in range(3):
        for x in range(12):
            at = 2 * (12 * c + x)
            yu[at : at + 2, :] = fine[c, x, 10:12, :]
            yd[at : at + 2, :] = fine[c, x, 0:2, :]
        for x in range(6):
            at = 72 + 2 * (6 * c + x)
            yu[at : at + 2, :] = coarse[c, x, 4:6, :]
            yd[at : at + 2, :] = coarse[c, x, 0:2, :]
    row = row_iota((16, 128))
    yu[GROW : GROW + 16, :] = jnp.where(row < 4, pltpu.roll(g, 16 - 6, 0), 0.0)
    yd[GROW : GROW + 16, :] = jnp.where((row >= 9) & (row < 13), pltpu.roll(g, 6, 0), 0.0)
    for ref in (yu, yd):
        ref[GROW + 16 : ROWS, :] = jnp.zeros((ROWS - GROW - 16, 128), F32)


def step_kernel(
    fine, prev, mu, coef, coarse, cprev, cmu, ccoef, gx, rxu, rxd, ryu, ryd,
    base, cnext, ghost, g_s, f_s, yf, yc,
):
    lane = lane_iota((16, 128))
    g_in = gx[...] + ryu[GROW : GROW + 16, :] + ryd[GROW : GROW + 16, :]
    only = jnp.where((lane >= 48) & (lane < 64), g_in, 0.0)
    inv = pltpu.roll(only, 128 - 48, 1) + pltpu.roll(only, 128 - 32, 1) + pltpu.roll(only, 128 - 16, 1)
    g = inv * g_in
    for _ in range(ITERS):
        t = (pltpu.roll(g, 1, 1) + pltpu.roll(g, 127, 1) + 6.0 * g) * 0.125
        t = (pltpu.roll(t, 1, 0) + pltpu.roll(t, 15, 0) + 6.0 * t) * 0.125
        g = inv * (g_in + t)
    g_s[...] = g
    turned = g.T
    for c in range(3):
        ghost[c] = turned[16 * c + 3 : 16 * c + 9, 3:9]
    for j in range(6):
        low = g_s[3 + j : 4 + j, :]
        f_s[2 * j : 2 * j + 1, :] = low
        f_s[2 * j + 1 : 2 * j + 2, :] = 0.5 * (low + g_s[4 + j : 5 + j, :])
    even = f_s[...][0:12]
    odd = 0.5 * (even + pltpu.roll(even, 127, 1))
    coarse_g = g_s[3:9, :]

    lane12 = lane_iota((12, 128))
    for c in range(3):
        for x in range(12):
            k = 12 * c + x
            yf[k, 0:2, :] = ryu[2 * k : 2 * k + 2, :]
            yf[k, 2:14, :] = fine[c, x]
            yf[k, 14:16, :] = ryd[2 * k : 2 * k + 2, :]
        for x in range(6):
            k = 6 * c + x
            yc[k, 0:2, :] = ryu[72 + 2 * k : 74 + 2 * k, :]
            yc[k, 2:8, :] = coarse[c, x]
            yc[k, 8:10, :] = ryd[72 + 2 * k : 74 + 2 * k, :]

    def fine_at(c, x):
        if x < 0:
            at = 18 * (2 * c + x + 2)
            return rxu[at : at + 12, :]
        if x >= 12:
            at = 18 * (2 * c + x - 12)
            return rxd[at : at + 12, :]
        return fine[c, x]

    def coarse_at(c, x):
        if x < 0:
            at = 18 * (2 * c + x + 2) + 12
            return rxu[at : at + 6, :]
        if x >= 6:
            at = 18 * (2 * c + x - 6) + 12
            return rxd[at : at + 6, :]
        return coarse[c, x]

    for x in range(12):
        cm = coef[x] * mu[x]
        for c in range(3):
            u = fine[c, x]
            k = 12 * c + x
            near = fine_at(c, x - 1) + fine_at(c, x + 1) + yf[k, 1:13, :] + yf[k, 3:15, :]
            far = fine_at(c, x - 2) + fine_at(c, x + 2) + yf[k, 0:12, :] + yf[k, 4:16, :]
            below = pltpu.roll(u, 127, 1)
            above = jnp.where(lane12 == 0, below, pltpu.roll(u, 1, 1))
            at = 16 * c + 3 + x // 2
            edge = (even if x % 2 == 0 else odd)[:, at : at + 1]
            below = jnp.where(lane12 == 127, edge, below)
            terms = (16.0 * near - far) * (1.0 / 12.0) - 7.0 * u + above + below
            base[c, x] = 2.0 * u - prev[c, x] + cm * terms
    lane6 = lane_iota((6, 128))
    for x in range(6):
        cm = 0.25 * (ccoef[x] * cmu[x])
        for c in range(3):
            u = coarse[c, x]
            k = 6 * c + x
            near = coarse_at(c, x - 1) + coarse_at(c, x + 1) + yc[k, 1:7, :] + yc[k, 3:9, :]
            far = coarse_at(c, x - 2) + coarse_at(c, x + 2) + yc[k, 0:6, :] + yc[k, 4:10, :]
            at = 16 * c + 3 + x
            above = jnp.where(lane6 == 0, coarse_g[:, at : at + 1], pltpu.roll(u, 1, 1))
            below = jnp.where(lane6 == 127, 0.0, pltpu.roll(u, 127, 1))
            terms = (16.0 * near - far) * (1.0 / 12.0) - 7.0 * u + above + below
            cnext[c, x] = 2.0 * u - cprev[c, x] + cm * terms


K = 32


def matrices(first, second):
    device = first >> 3
    row, half = row_of(device)
    pick = jnp.where(lane_iota((K, ROWS_ALL)) == row, 1.0, 0.0)
    lanes = lane_iota((K, 128))
    base_lane = 64 * half + (first & 7)
    z = second & 127
    live = first >= 0
    here = jnp.where((lanes == z) & live, 1.0, 0.0)
    step = jnp.where((lanes == z + 1) & live, 1.0, 0.0) - jnp.where((lanes == z - 1) & live, 1.0, 0.0)
    lx = (second >> 11) - 1
    ly = ((second >> 7) & 15) - 1
    at = 16 * lx + ly
    place = lane_iota((K, 256))
    along_x = jnp.where(place == at + 16, 1.0, 0.0) - jnp.where(place == at - 16, 1.0, 0.0)
    along_y = jnp.where(place == at + 1, 1.0, 0.0) - jnp.where(place == at - 1, 1.0, 0.0)
    centre = jnp.where(place == at, 1.0, 0.0)
    spread = jnp.concatenate([along_x, along_y, centre, jnp.zeros((128 - 3 * K, 256), F32)], axis=0)
    return pick, jnp.broadcast_to(base_lane, (K, 128)), here, step, spread.T


def columns(number, rank, first, second):
    want = (row_iota((K, 128)) + number * K).astype(F32)
    one = jnp.zeros((K, 128), F32)
    two = jnp.zeros((K, 128), F32)
    for r in range(32):
        same = rank[r : r + 1, :] == want
        one = one + jnp.where(same, first[r : r + 1, :], 0.0)
        two = two + jnp.where(same, second[r : r + 1, :], 0.0)
    one = jnp.sum(one, axis=1, keepdims=True).astype(jnp.int32) - 1
    two = jnp.sum(two, axis=1, keepdims=True).astype(jnp.int32)
    return one, two


def find_kernel(start, cells, count, rank, first, second, pick, base_lane, here, step, spread, hit_s):
    lane = lane_iota((1, 128))
    for r in range(32):
        part = cells[:, 128 * r : 128 * (r + 1)]
        lx = part[0:1, :] - start[0]
        ly = part[1:2, :] - start[1]
        inside = (lx >= -1) & (lx <= 12) & (ly >= -1) & (ly <= 12)
        hit_s[r : r + 1, :] = jnp.where(inside, 1.0, 0.0)
        first[r : r + 1, :] = (lane + (128 * r + 1)).astype(F32)
        second[r : r + 1, :] = (((lx + 1) << 11) + ((ly + 1) << 7) + part[2:3, :]).astype(F32)
    hit = hit_s[...]
    square = (128, 128)
    before = jnp.where(row_iota(square) < lane_iota(square), 1.0, 0.0)
    within = jnp.dot(hit, before, preferred_element_type=F32)
    total = jnp.dot(hit, jnp.ones(square, F32), preferred_element_type=F32)
    above = jnp.where(lane_iota((32, 32)) < row_iota((32, 32)), 1.0, 0.0)
    earlier = jnp.dot(above, total, preferred_element_type=F32)
    rank[...] = jnp.where(hit > 0.0, within + earlier, -1.0)
    count[0] = jnp.sum(hit).astype(jnp.int32)
    one, two = columns(0, rank, first, second)
    pick[...], base_lane[...], here[...], step[...], spread[...] = matrices(one, two)


def source_kernel(count, rank, first, second, pick, base_lane, here, step, spread, base, coef, rows, out):
    def add(source, pick, base_lane, here, step, spread):
        line = jnp.dot(pick, rows[...], precision=lax.Precision.HIGHEST, preferred_element_type=F32)
        lanes = lane_iota((K, 128)) - base_lane
        m = [
            0.5 * jnp.sum(jnp.where(lanes == 8 * i, line, 0.0), axis=1, keepdims=True) for i in range(6)
        ]
        pad = jnp.zeros((128 - 3 * K, 128), F32)
        wide = []
        for a, b, c in ((0, 3, 4), (3, 1, 5), (4, 5, 2)):
            wide.append(jnp.concatenate([m[a] * here, m[b] * here, m[c] * step, pad], axis=0))
        wide = jnp.concatenate(wide, axis=1)
        force = jnp.dot(spread, wide, precision=lax.Precision.HIGHEST, preferred_element_type=F32)
        for x in range(12):
            for c in range(3):
                out[c, x] = source[c, x] + coef[x] * force[16 * x : 16 * x + 12, 128 * c : 128 * (c + 1)]

    add(base, pick[...], base_lane[...], here[...], step[...], spread[...])

    def more(number, carry):
        one, two = columns(number, rank, first, second)
        add(out, *matrices(one, two))
        return carry

    lax.fori_loop(1, (count[0] + K - 1) // K, more, 0)


TWO = False
IDS = np.arange(512).reshape(8, 8, 8)
STAGE1 = IDS.transpose(0, 2, 1).reshape(64, 8).tolist()
STAGE2 = IDS.transpose(1, 0, 2).reshape(8, 64).tolist()
ROWS_ALL = 256 if TWO else 512


def row_of(d):
    if not TWO:
        return d, 0
    first = (d >> 3) & 7
    second = ((d >> 6) << 3) | (d & 7)
    return second * 4 + (first >> 1), first & 1


def shape(*dims):
    return jax.ShapeDtypeStruct(dims, F32)


def shifted(x, axis, step):
    size = lax.axis_size(axis)
    pairs = [(i, i + step) for i in range(size) if 0 <= i + step < size]
    return lax.ppermute(x, axis, pairs)


def local(
    fine_now, fine_prev, fine_mu, fine_coef, coarse_now, coarse_prev, coarse_mu, coarse_coef, src_cell, src_moment,
):
    ix = lax.axis_index("gx")
    iy = lax.axis_index("gy")
    device = ix * 16 + iy
    half = (row_of(device)[1] + 0 * device).astype(jnp.int32).reshape(1)
    start = jnp.stack([ix * 12, iy * 12]).astype(jnp.int32)
    params = pltpu.CompilerParams(vmem_limit_bytes=32 * 1024 * 1024)

    xu, xd, own, row = pl.pallas_call(
        pack_x_kernel,
        in_specs=vspec(4) + [pl.BlockSpec(memory_space=SMEM)],
        out_specs=vspec(4),
        out_shape=[shape(ROWS, 128), shape(ROWS, 128), shape(16, 128), shape(8 if TWO else 512, 128)],
        scratch_shapes=[VMEM((24, 128), F32), VMEM((16, 128), F32)],
        compiler_params=params,
        name="pack_x",
    )(fine_now, coarse_now, coarse_mu, src_moment, half)
    if TWO:
        first = lax.all_to_all(row.reshape(8, 1, 128), AX, 0, 0, tiled=True, axis_index_groups=STAGE1)
    else:
        gathered = lax.all_to_all(row.reshape(512, 1, 128), AX, 0, 0, tiled=True)
    rxu = shifted(xu, "gx", 1)
    rxd = shifted(xd, "gx", -1)
    found = pl.pallas_call(
        find_kernel,
        in_specs=[pl.BlockSpec(memory_space=SMEM), pl.BlockSpec(memory_space=VMEM)],
        out_specs=[pl.BlockSpec(memory_space=SMEM)] + vspec(8),
        out_shape=[
            jax.ShapeDtypeStruct((1,), jnp.int32),
            shape(32, 128), shape(32, 128), shape(32, 128), shape(K, ROWS_ALL),
            jax.ShapeDtypeStruct((K, 128), jnp.int32),
            shape(K, 128), shape(K, 128), shape(256, 128),
        ],
        scratch_shapes=[VMEM((32, 128), F32)],
        compiler_params=params,
        name="find_sources",
    )(start, src_cell)
    yu, yd, gx = pl.pallas_call(
        pack_y_kernel,
        in_specs=vspec(5),
        out_specs=vspec(3),
        out_shape=[shape(ROWS, 128), shape(ROWS, 128), shape(16, 128)],
        compiler_params=params,
        name="pack_y",
    )(fine_now, coarse_now, own, rxu, rxd)
    ryu = shifted(yu, "gy", 1)
    ryd = shifted(yd, "gy", -1)
    if TWO:
        packed = jnp.sum(first.reshape(4, 2, 128), axis=1)
        gathered = lax.all_to_all(
            jnp.broadcast_to(packed[None], (64, 4, 128)), AX, 0, 0, tiled=True, axis_index_groups=STAGE2
        )
    base, cnext, ghost = pl.pallas_call(
        step_kernel,
        in_specs=vspec(13),
        out_specs=vspec(3),
        out_shape=[shape(3, 12, 12, 128), shape(3, 6, 6, 128), shape(3, 6, 6)],
        scratch_shapes=[
            VMEM((16, 128), F32),
            VMEM((16, 128), F32),
            VMEM((36, 16, 128), F32),
            VMEM((18, 16, 128), F32),
        ],
        compiler_params=params,
        name="step",
    )(
        fine_now, fine_prev, fine_mu, fine_coef, coarse_now, coarse_prev, coarse_mu, coarse_coef,
        gx, rxu, rxd, ryu, ryd,
    )
    fine_next = pl.pallas_call(
        source_kernel,
        in_specs=[pl.BlockSpec(memory_space=SMEM)] + vspec(11),
        out_specs=pl.BlockSpec(memory_space=VMEM),
        out_shape=shape(3, 12, 12, 128),
        compiler_params=params,
        name="add_sources",
    )(*found, base, fine_coef, gathered.reshape(ROWS_ALL, 128))
    return fine_next, cnext, ghost


def solution(mesh):
    in_specs = (
        P(None, "gx", "gy", None),
        P(None, "gx", "gy", None),
        P("gx", "gy", None),
        P("gx", "gy", None),
        P(None, "gx", "gy", None),
        P(None, "gx", "gy", None),
        P("gx", "gy", None),
        P("gx", "gy", None),
        P(),
        P(None, ("gx", "gy")),
    )
    out_specs = (P(None, "gx", "gy", None), P(None, "gx", "gy", None), P(None, "gx", "gy"))
    return jax.shard_map(local, mesh=mesh, in_specs=in_specs, out_specs=out_specs, check_vma=False)
```

time: 1790 us -> 56 us (0.03)
  the two profiles are of different devices: /device:TPU:34 before, /device:TPU:31 now
where the time goes in v1:
time: 56 us; the launch traced here: 55.6 us
  starting transfers between devices  38.1 us (68%)
  waiting for transfers between devices  7.24 us (13%)
  Pallas kernels  6.07 us (11%)
  local copies, waits for them, and re-layouts  3.3 us (6%)
  between operations  0.81 us (1%)
    all_to_all x1, starting transfers between devices, local(): gathered = lax.all_to_all(row.reshape(512, 1, 128), AX, 0, 0, tiled=True)  21.2 us
    ppermute x4, starting transfers between devices, shifted(): return lax.ppermute(x, axis, pairs)  16.9 us
    ppermute x4, waiting for transfers between devices, shifted(): return lax.ppermute(x, axis, pairs)  7.24 us
    unnamed x26, local copies, waits for them, and re-layouts  3.3 us
    pallas_call x1, Pallas kernels, local(): pl.pallas_call(source_kernel, in_specs=[pl.BlockSpec(memory_space=SMEM)]...  2.13 us
    pallas_call x1, Pallas kernels, local(): pl.pallas_call(find_kernel, in_specs=[pl.BlockSpec(memory_space=SMEM), pl...  1.61 us
    pallas_call x1, Pallas kernels, local(): pl.pallas_call(step_kernel, in_specs=vspec(13), out_specs=vspec(3), out_s...  1.29 us
  transfers between devices with their start and end apart: 5, of which 1 were waited for; matrix products, arithmetic and copies ran while one was open for 0% of the time, Pallas kernels for 5%

profile of v1, /device:TPU:31, one launch (start us, length us, event | category | flops | bytes accessed | tf_op | source)
XLA Modules:
  0.0 55.6 jit_solution(2935972059871049827)
XLA Ops:
  0.6 0.0 copy-start
  0.6 1.0 %copy-done = f32[3,12,12,128]{3,2,1,0:T(8,128)S(1)} copy-done((f32[3,12,12,128]{3,2,1,0:T(8,128)S(1)}, f32[3,12,12,128]{3,2,1,0:T(8,128)}, u32[]{:S(2)}) %copy-start) | copy-done | bytes 221208
  1.6 0.9 %copy-done.2 = f32[3,6,6,128]{3,2,1,0:T(8,128)S(1)} copy-done((f32[3,6,6,128]{3,2,1,0:T(8,128)S(1)}, f32[3,6,6,128]{3,2,1,0:T(8,128)}, u32[]{:S(2)}) %copy-start.2) | copy-done | bytes 55320
  2.5 0.7 %copy-done.7 = f32[6,6,128]{2,1,0:T(8,128)S(1)} copy-done((f32[6,6,128]{2,1,0:T(8,128)S(1)}, f32[6,6,128]{2,1,0:T(8,128)}, u32[]{:S(2)}) %copy-start.7) | copy-done | bytes 18456
  3.2 0.7 %copy-done.12 = f32[6,8]{1,0:T(8,128)S(1)} copy-done((f32[6,8]{1,0:T(8,128)S(1)}, f32[6,8]{1,0:T(8,128)}, u32[]{:S(2)}) %copy-start.12) | copy-done | bytes 216
  3.9 1.0 %pack_x.1 = (f32[128,128]{1,0:T(8,128)S(1)}, f32[128,128]{1,0:T(8,128)S(1)}, f32[16,128]{1,0:T(8,128)S(1)}, f32[512,128]{1,0:T(8,128)}) custom-call(f32[3,12,12,128]{3,2,1,0:T(8,128)S(1)} %copy-done, f32[3,6,6,128]{3,2,1,0:T(8,128)S(1)} %copy-done.2, f32[6,6,128]{2,1,0:T(8,128)S(1)} %copy-done.7, f32[6,8]{1,0:T(8,128)S(1)} %copy-done.12, s32[1]{0:T(128)} %constant.12.clone.1.half), custom_call_target="tpu_custom_call" | custom-call | tf_op jit(solution)/shard_map/pack_x/pallas_call | solution.py:310
  4.9 21.2 %all-to-all-start = ((f32[512,1,128]{2,1,0:T(1,128)}), f32[512,1,128]{2,1,0:T(1,128)S(1)}, u32[]{:S(2)}, u32[]{:S(2)}) async-start(f32[512,1,128]{2,1,0:T(1,128)} %bitcast.3), calls=%async_computation | async-start | bytes 524288 | tf_op jit(solution)/shard_map/all_to_all | solution.py:322
  26.1 5.5 %collective-permute-start = (f32[128,128]{1,0:T(8,128)S(1)}, f32[128,128]{1,0:T(8,128)S(1)}, u32[]{:S(2)}, u32[]{:S(2)}) collective-permute-start(f32[128,128]{1,0:T(8,128)S(1)} %get-tuple-element.32), channel_id=1, source_target_pairs={{0,16},{16,32},{32,48},{48,64},{64,80},{80,96},{96,112},{112,128},... | collective-permute-start | bytes 196616 | tf_op jit(solution)/shard_map/ppermute | solution.py:297
  31.6 1.9 %collective-permute-start.1 = (f32[128,128]{1,0:T(8,128)S(1)}, f32[128,128]{1,0:T(8,128)S(1)}, u32[]{:S(2)}, u32[]{:S(2)}) collective-permute-start(f32[128,128]{1,0:T(8,128)S(1)} %get-tuple-element.33), channel_id=1, source_target_pairs={{16,0},{32,16},{48,32},{64,48},{80,64},{96,80},{112,96},{128,112},... | collective-permute-start | bytes 196616 | tf_op jit(solution)/shard_map/ppermute | solution.py:297
  33.6 0.0 copy-start.9
  33.6 0.0 copy-start.5
  33.6 0.0 collective-permute-done.rxu
  33.6 7.2 %collective-permute-done.1.rxd = f32[128,128]{1,0:T(8,128)S(1)} collective-permute-done((f32[128,128]{1,0:T(8,128)S(1)}, f32[128,128]{1,0:T(8,128)S(1)}, u32[]{:S(2)}, u32[]{:S(2)}) %collective-permute-start.1) | collective-permute-done | bytes 65568 | tf_op jit(solution)/shard_map/ppermute | solution.py:297
  40.8 0.0 copy-done.1
  40.8 0.0 copy-done.3
  40.9 3.8 %collective-permute-start.2 = (f32[128,128]{1,0:T(8,128)S(1)}, f32[128,128]{1,0:T(8,128)S(1)}, u32[]{:S(2)}, u32[]{:S(2)}) collective-permute-start(f32[128,128]{1,0:T(8,128)S(1)} %get-tuple-element.35), channel_id=1, source_target_pairs={{0,1},{1,2},{2,3},{3,4},{4,5},{5,6},{6,7},{7,8},{8,9},{9,10},{10,1... | collective-permute-start | bytes 196616 | tf_op jit(solution)/shard_map/ppermute | solution.py:297
  44.7 5.7 %collective-permute-start.3 = (f32[128,128]{1,0:T(8,128)S(1)}, f32[128,128]{1,0:T(8,128)S(1)}, u32[]{:S(2)}, u32[]{:S(2)}) collective-permute-start(f32[128,128]{1,0:T(8,128)S(1)} %get-tuple-element.36), channel_id=1, source_target_pairs={{1,0},{2,1},{3,2},{4,3},{5,4},{6,5},{7,6},{8,7},{9,8},{10,9},{11,1... | collective-permute-start | bytes 196616 | tf_op jit(solution)/shard_map/ppermute | solution.py:297
  50.4 0.1 pad_add_fusion.start
  50.5 1.6 %find_sources.1 = (s32[1]{0:T(128)}, f32[32,128]{1,0:T(8,128)S(1)}, f32[32,128]{1,0:T(8,128)S(1)}, f32[32,128]{1,0:T(8,128)S(1)}, f32[32,512]{1,0:T(8,128)S(1)},...) custom-call(s32[2]{0:T(128)S(1)} %pad_add_fusion.start, ...), custom_call_target="tpu_custom_call" | custom-call | tf_op jit(solution)/shard_map/find_sources/pallas_call | solution.py:325
  52.1 0.0 collective-permute-done.2.ryu
  52.1 0.0 collective-permute-done.3.ryd
  52.2 1.3 %step.1 = (f32[3,12,12,128]{3,2,1,0:T(8,128)S(1)}, f32[3,6,6,128]{3,2,1,0:T(8,128)}, f32[3,6,6]{2,1,0:T(8,128)}) custom-call(f32[3,12,12,128]{3,2,1,0:T(8,128)S(1)} %copy-done.1, f32[3,12,12,128]{3,2,1,0:T(8,128)S(1)} %copy-done.5, f32[12,12,128]{2,1,0:T(8,128)S(1)} %copy-done.6, f32[12,12,128]{2,1,0:T(8,128)S(1)} %copy-done.4, ...), custom_call_target="tpu_custom_call" | custom-call | tf_op jit(solution)/shard_map/step/pallas_call | solution.py:354
  53.5 0.0 all-to-all-done
  53.5 2.1 %add_sources.1 = f32[3,12,12,128]{3,2,1,0:T(8,128)} custom-call(s32[1]{0:T(128)} %get-tuple-element.22.count, f32[32,128]{1,0:T(8,128)S(1)} %get-tuple-element.23.rank, f32[32,128]{1,0:T(8,128)S(1)} %get-tuple-element.24.first, f32[32,128]{1,0:T(8,128)S(1)} %get-tuple-element.25.second, f32[32,512]{1,0:T(8,128)S(1)} %get-tuple-element.26.pick, ...), custom_call_target="tpu_custom_call" | custom-call | tf_op jit(solution)/shard_map/add_sources/pallas_call | solution.py:371
  (18 shorter events, 0.1 us)
Async XLA Ops:
  0.6 1.0 %copy-start = (f32[3,12,12,128]{3,2,1,0:T(8,128)S(1)}, f32[3,12,12,128]{3,2,1,0:T(8,128)}, u32[]{:S(2)}) copy-start(f32[3,12,12,128]{3,2,1,0:T(8,128)} %fine.5) | copy-start | bytes 663556
  1.6 0.9 %copy-start.2 = (f32[3,6,6,128]{3,2,1,0:T(8,128)S(1)}, f32[3,6,6,128]{3,2,1,0:T(8,128)}, u32[]{:S(2)}) copy-start(f32[3,6,6,128]{3,2,1,0:T(8,128)} %coarse.5) | copy-start | bytes 165892
  2.5 0.7 %copy-start.7 = (f32[6,6,128]{2,1,0:T(8,128)S(1)}, f32[6,6,128]{2,1,0:T(8,128)}, u32[]{:S(2)}) copy-start(f32[6,6,128]{2,1,0:T(8,128)} %cmu.1) | copy-start | bytes 55300
  3.2 0.7 %copy-start.12 = (f32[6,8]{1,0:T(8,128)S(1)}, f32[6,8]{1,0:T(8,128)}, u32[]{:S(2)}) copy-start(f32[6,8]{1,0:T(8,128)} %mom.1) | copy-start | bytes 580
  4.9 35.9 %copy-start.1 = (f32[3,12,12,128]{3,2,1,0:T(8,128)S(1)}, f32[3,12,12,128]{3,2,1,0:T(8,128)}, u32[]{:S(2)}) copy-start(f32[3,12,12,128]{3,2,1,0:T(8,128)} %fine.5) | copy-start | bytes 663556
  4.9 35.9 %copy-start.3 = (f32[3,6,6,128]{3,2,1,0:T(8,128)S(1)}, f32[3,6,6,128]{3,2,1,0:T(8,128)}, u32[]{:S(2)}) copy-start(f32[3,6,6,128]{3,2,1,0:T(8,128)} %coarse.5) | copy-start | bytes 165892
  4.9 45.6 %copy-start.10 = (s32[3,4096]{1,0:T(4,128)S(1)}, s32[3,4096]{1,0:T(4,128)}, u32[]{:S(2)}) copy-start(s32[3,4096]{1,0:T(4,128)} %cells.1) | copy-start | bytes 147460
  4.9 47.2 %copy-start.11 = (f32[6,6,128]{2,1,0:T(8,128)S(1)}, f32[6,6,128]{2,1,0:T(8,128)}, u32[]{:S(2)}) copy-start(f32[6,6,128]{2,1,0:T(8,128)} %ccoef.1) | copy-start | bytes 55300
  4.9 48.6 %all-to-all-start = ((f32[512,1,128]{2,1,0:T(1,128)}), f32[512,1,128]{2,1,0:T(1,128)S(1)}, u32[]{:S(2)}, u32[]{:S(2)}) async-start(f32[512,1,128]{2,1,0:T(1,128)} %bitcast.3), calls=%async_computation | async-start | bytes 524288 | tf_op jit(solution)/shard_map/all_to_all | solution.py:322
  26.1 7.5 %collective-permute-start = (f32[128,128]{1,0:T(8,128)S(1)}, f32[128,128]{1,0:T(8,128)S(1)}, u32[]{:S(2)}, u32[]{:S(2)}) collective-permute-start(f32[128,128]{1,0:T(8,128)S(1)} %get-tuple-element.32), channel_id=1, source_target_pairs={{0,16},{16,32},{32,48},{48,64},{64,80},{80,96},{96,112},{112,128},... | collective-permute-start | bytes 196616 | tf_op jit(solution)/shard_map/ppermute | solution.py:297
  31.6 9.2 %collective-permute-start.1 = (f32[128,128]{1,0:T(8,128)S(1)}, f32[128,128]{1,0:T(8,128)S(1)}, u32[]{:S(2)}, u32[]{:S(2)}) collective-permute-start(f32[128,128]{1,0:T(8,128)S(1)} %get-tuple-element.33), channel_id=1, source_target_pairs={{16,0},{32,16},{48,32},{64,48},{80,64},{96,80},{112,96},{128,112},... | collective-permute-start | bytes 196616 | tf_op jit(solution)/shard_map/ppermute | solution.py:297
  33.6 18.6 %copy-start.9 = (f32[3,6,6,128]{3,2,1,0:T(8,128)S(1)}, f32[3,6,6,128]{3,2,1,0:T(8,128)}, u32[]{:S(2)}) copy-start(f32[3,6,6,128]{3,2,1,0:T(8,128)} %cprev.1) | copy-start | bytes 165892
  33.6 18.6 %copy-start.5 = (f32[3,12,12,128]{3,2,1,0:T(8,128)S(1)}, f32[3,12,12,128]{3,2,1,0:T(8,128)}, u32[]{:S(2)}) copy-start(f32[3,12,12,128]{3,2,1,0:T(8,128)} %prev.1) | copy-start | bytes 663556
  40.8 11.3 %copy-start.4 = (f32[12,12,128]{2,1,0:T(8,128)S(1)}, f32[12,12,128]{2,1,0:T(8,128)}, u32[]{:S(2)}) copy-start(f32[12,12,128]{2,1,0:T(8,128)} %coef.3) | copy-start | bytes 221188
  40.8 11.3 %copy-start.6 = (f32[12,12,128]{2,1,0:T(8,128)S(1)}, f32[12,12,128]{2,1,0:T(8,128)}, u32[]{:S(2)}) copy-start(f32[12,12,128]{2,1,0:T(8,128)} %mu.3) | copy-start | bytes 221188
  40.9 11.2 %collective-permute-start.2 = (f32[128,128]{1,0:T(8,128)S(1)}, f32[128,128]{1,0:T(8,128)S(1)}, u32[]{:S(2)}, u32[]{:S(2)}) collective-permute-start(f32[128,128]{1,0:T(8,128)S(1)} %get-tuple-element.35), channel_id=1, source_target_pairs={{0,1},{1,2},{2,3},{3,4},{4,5},{5,6},{6,7},{7,8},{8,9},{9,10},{10,1... | collective-permute-start | bytes 196616 | tf_op jit(solution)/shard_map/ppermute | solution.py:297
  44.7 7.5 %collective-permute-start.3 = (f32[128,128]{1,0:T(8,128)S(1)}, f32[128,128]{1,0:T(8,128)S(1)}, u32[]{:S(2)}, u32[]{:S(2)}) collective-permute-start(f32[128,128]{1,0:T(8,128)S(1)} %get-tuple-element.36), channel_id=1, source_target_pairs={{1,0},{2,1},{3,2},{4,3},{5,4},{6,5},{7,6},{8,7},{9,8},{10,9},{11,1... | collective-permute-start | bytes 196616 | tf_op jit(solution)/shard_map/ppermute | solution.py:297
  50.5 1.7 %copy-start.8 = (f32[6,6,128]{2,1,0:T(8,128)S(1)}, f32[6,6,128]{2,1,0:T(8,128)}, u32[]{:S(2)}) copy-start(f32[6,6,128]{2,1,0:T(8,128)} %cmu.1) | copy-start | bytes 55300

commit v2 on v1

v2 whole, which is shorter than its diff:
```python
import jax
import jax.numpy as jnp
from jax import lax
from jax.experimental import pallas as pl
from jax.experimental.pallas import tpu as pltpu
from jax.sharding import PartitionSpec as P

ITERS = 3
NX, NY = 32, 16
FIRST_LIMIT = 60 * 1024 * 1024
AX = ("gx", "gy")
ROWS = 160
GROW = 108
ROWS_X = 160
GROW_X = 144
VMEM = pltpu.VMEM
F32 = jnp.float32


def vspec(n):
    return [pl.BlockSpec(memory_space=VMEM)] * n


def lane_iota(shape):
    return lax.broadcasted_iota(jnp.int32, shape, len(shape) - 1)


def row_iota(shape):
    return lax.broadcasted_iota(jnp.int32, shape, 0)


def interface_piece(fine, coarse, mu, a_s, g_s, ready):
    lane = lane_iota((1, 128))
    b = jnp.zeros((6, 128), F32)
    ready(3)
    ready(4)
    for i in range(6):
        for c in range(3):
            col = 2.0 * coarse[c, i, :, 0:1] - coarse[c, i, :, 1:2]
            b = b + jnp.where(lane == c * 16 + 3 + i, col, 0.0)
        inv = 1.0 / (0.6 + mu[i, :, 0:1])
        b = b + jnp.where(lane == 48 + 3 + i, inv, 0.0)
    acc = jnp.zeros((12, 128), F32)
    for c in range(3):
        ready(c)
        for x in range(12):
            at = c * 16 + 3 + x // 2
            if x % 2 == 0:
                w = jnp.where(lane == at, 0.5, 0.0)
            else:
                w = jnp.where((lane == at) | (lane == at + 1), 0.25, 0.0)
            acc = acc + fine[c, x, :, 126:127] * w
    a_s[...] = jnp.zeros((24, 128), F32)
    a_s[1:13, :] = acc
    g_s[...] = jnp.zeros((16, 128), F32)
    for j in range(7):
        g_s[3 + j : 4 + j, :] = (
            0.25 * a_s[2 * j : 2 * j + 1, :]
            + 0.5 * a_s[2 * j + 1 : 2 * j + 2, :]
            + 0.25 * a_s[2 * j + 2 : 2 * j + 3, :]
        )
    g_s[3:9, :] = g_s[3:9, :] + b


def rows_kernel(fine_hbm, coarse_hbm, mu_hbm, mom_hbm, rows, a_s, g_s, fine, coarse, mu, mom, sems):
    copies = [pltpu.make_async_copy(fine_hbm.at[c], fine.at[c], sems.at[c]) for c in range(3)]
    copies.append(pltpu.make_async_copy(coarse_hbm, coarse, sems.at[3]))
    copies.append(pltpu.make_async_copy(mu_hbm, mu, sems.at[4]))
    copies.append(pltpu.make_async_copy(mom_hbm, mom, sems.at[5]))
    for n in (5, 3, 4, 0, 1, 2):
        copies[n].start()
    lane = lane_iota((1, 128))
    lanes = lane_iota((6, 128))
    want = 8 * row_iota((6, 128)) + 64
    t = jnp.zeros((6, 128), F32)
    copies[5].wait()
    for j in range(8):
        t = t + jnp.where(lanes == want + j, mom[:, j : j + 1], 0.0)
    row = jnp.sum(t, axis=0, keepdims=True)
    rows[...] = jnp.broadcast_to(row, rows.shape)
    interface_piece(fine, coarse, mu, a_s, g_s, lambda n: copies[n].wait())
    ix = lax.axis_index("gx")
    iy = lax.axis_index("gy")
    for a in (1, -1):
        for b in (1, -1):
            from_x, from_y = 6 if a > 0 else 3, 6 if b > 0 else 3
            corner = row
            for j in range(4):
                line = pltpu.roll(g_s[from_y + j : from_y + j + 1, :], (128 + 4 * j - from_x) % 128, 1)
                corner = corner + jnp.where((lane < 64) & ((lane & 15) // 4 == j), line, 0.0)

            @pl.when(inside(ix + a, iy + b))
            def _():
                rows[pl.ds((ix + a) * NY + iy + b, 1), :] = corner


def pack_kernel(fine, coarse, mu, own, xa, xb, ya, yb, a_s, g_s):
    interface_piece(fine, coarse, mu, a_s, g_s, lambda n: None)
    g = g_s[...]
    own[...] = g
    odd_x = (lax.axis_index("gx") & 1) == 1
    odd_y = (lax.axis_index("gy") & 1) == 1

    def put(refs, odd, rows, up, down):
        one, two = refs
        one[rows, :] = jnp.where(odd, down, up)
        two[rows, :] = jnp.where(odd, up, down)

    for c in range(3):
        for j in range(2):
            at = 24 * (2 * c + j)
            put((xa, xb), odd_x, slice(at, at + 12), fine[c, 10 + j], fine[c, j])
            put((xa, xb), odd_x, slice(at + 16, at + 22), coarse[c, 4 + j], coarse[c, j])
        for x in range(12):
            at = 2 * (12 * c + x)
            put((ya, yb), odd_y, slice(at, at + 2), fine[c, x, 10:12, :], fine[c, x, 0:2, :])
        for x in range(6):
            at = 72 + 2 * (6 * c + x)
            put((ya, yb), odd_y, slice(at, at + 2), coarse[c, x, 4:6, :], coarse[c, x, 0:2, :])
    place = lane_iota((16, 128)) & 15
    row = row_iota((16, 128))
    here = slice(GROW, GROW + 16)
    up = jnp.where(place < 4, pltpu.roll(g, 128 - 6, 1), 0.0)
    down = jnp.where((place >= 9) & (place < 13), pltpu.roll(g, 6, 1), 0.0)
    put((xa, xb), odd_x, slice(GROW_X, ROWS_X), up, down)
    up = jnp.where(row < 4, pltpu.roll(g, 16 - 6, 0), 0.0)
    down = jnp.where((row >= 9) & (row < 13), pltpu.roll(g, 6, 0), 0.0)
    put((ya, yb), odd_y, here, up, down)
    for ref in (ya, yb):
        ref[GROW + 16 : ROWS, :] = jnp.zeros((ROWS - GROW - 16, 128), F32)


def inside(x, y):
    return (x >= 0) & (x < NX) & (y >= 0) & (y < NY)


def lower(rows, one, two, odd):
    return jnp.where(odd, one[rows, :], two[rows, :])


def upper(rows, one, two, odd):
    return jnp.where(odd, two[rows, :], one[rows, :])


def base_kernel(fine, prev, mu, coef, coarse, cprev, cmu, ccoef, ya, yb, base, cbase, yf, yc):
    odd_y = (lax.axis_index("gy") & 1) == 1

    def terms(field, pad, c, x, at, size, edge):
        u = field[c, x]
        k = size * c + x
        rows = slice(at + 2 * k, at + 2 * k + 2)
        pad[k, 0:2, :] = lower(rows, ya, yb, odd_y)
        pad[k, 2 : size + 2, :] = u
        pad[k, size + 2 : size + 4, :] = upper(rows, ya, yb, odd_y)
        near = pad[k, 1 : size + 1, :] + pad[k, 3 : size + 3, :]
        far = pad[k, 0:size, :] + pad[k, 4 : size + 4, :]
        for d in (-1, 1):
            if 0 <= x + d < size:
                near = near + field[c, x + d]
            if 0 <= x + 2 * d < size:
                far = far + field[c, x + 2 * d]
        below = pltpu.roll(u, 127, 1)
        above = pltpu.roll(u, 1, 1)
        lane = lane_iota((size, 128))
        above = jnp.where(lane == 0, below if edge else 0.0, above)
        below = jnp.where(lane == 127, 0.0, below)
        return u, (16.0 * near - far) * (1.0 / 12.0) - 7.0 * u + above + below

    for x in range(12):
        cm = coef[x] * mu[x]
        for c in range(3):
            u, t = terms(fine, yf, c, x, 0, 12, True)
            base[c, x] = 2.0 * u - prev[c, x] + cm * t
    for x in range(6):
        cm = 0.25 * (ccoef[x] * cmu[x])
        for c in range(3):
            u, t = terms(coarse, yc, c, x, 72, 6, False)
            cbase[c, x] = 2.0 * u - cprev[c, x] + cm * t


def finish_kernel(
    pick, rank, first, second, base_lane, here, step, spread,
    base, cbase, mu, coef, cmu, ccoef, own, ya, yb, xb, xa, rows,
    fnext, cnext, ghost, g_s, f_s, force,
):
    lane = lane_iota((16, 128))
    line = lane_iota((1, 128))
    force[...] = source_force(rows, pick[...], base_lane[...], here[...], step[...], spread[...])
    g_s[...] = own[...]
    for ref, at in ((ya, GROW), (yb, GROW), (xa, GROW_X), (xb, GROW_X)):
        g_s[...] = g_s[...] + ref[at : at + 16, :]
    ix = lax.axis_index("gx")
    iy = lax.axis_index("gy")
    for a in (1, -1):
        for b in (1, -1):
            ok = inside(ix + a, iy + b)
            at = jnp.where(ok, (ix + a) * NY + iy + b, 0)
            corner = jnp.where(ok, rows[pl.ds(at, 1), :], 0.0)
            to_x, to_y = 9 if a > 0 else 0, 9 if b > 0 else 0
            keep = (line < 64) & ((line & 15) >= to_x) & ((line & 15) < to_x + 4)
            for j in range(4):
                part = jnp.where(keep, pltpu.roll(corner, (128 + to_x - 4 * j) % 128, 1), 0.0)
                g_s[to_y + j : to_y + j + 1, :] = g_s[to_y + j : to_y + j + 1, :] + part
    g_in = g_s[...]
    only = jnp.where((lane >= 48) & (lane < 64), g_in, 0.0)
    inv = pltpu.roll(only, 128 - 48, 1) + pltpu.roll(only, 128 - 32, 1) + pltpu.roll(only, 128 - 16, 1)
    g = inv * g_in
    for _ in range(ITERS):
        t = (pltpu.roll(g, 1, 1) + pltpu.roll(g, 127, 1) + 6.0 * g) * 0.125
        t = (pltpu.roll(t, 1, 0) + pltpu.roll(t, 15, 0) + 6.0 * t) * 0.125
        g = inv * (g_in + t)
    g_s[...] = g
    turned = g.T
    for c in range(3):
        ghost[c] = turned[16 * c + 3 : 16 * c + 9, 3:9]
    for j in range(6):
        low = g_s[3 + j : 4 + j, :]
        f_s[2 * j : 2 * j + 1, :] = low
        f_s[2 * j + 1 : 2 * j + 2, :] = 0.5 * (low + g_s[4 + j : 5 + j, :])
    even = f_s[0:12, :]
    odd = 0.5 * (even + pltpu.roll(even, 127, 1))
    coarse_g = g_s[3:9, :]
    def more(number, carry):
        force[...] = force[...] + source_force(rows, *matrices(*columns(number, rank, first, second)))
        return carry

    found = jnp.max(rank[...]).astype(jnp.int32) + 1
    lax.fori_loop(1, (found + K - 1) // K, more, 0)

    odd_x = (ix & 1) == 1

    def halo(c, x, at, size):
        low = [lower(slice(n + at, n + at + size), xa, xb, odd_x) for n in (48 * c, 48 * c + 24)]
        high = [upper(slice(n + at, n + at + size), xa, xb, odd_x) for n in (48 * c, 48 * c + 24)]
        if x == 0:
            return (16.0 * low[1] - low[0]) * (1.0 / 12.0)
        if x == 1:
            return low[1] * (-1.0 / 12.0)
        if x == size - 2:
            return high[0] * (-1.0 / 12.0)
        if x == size - 1:
            return (16.0 * high[0] - high[1]) * (1.0 / 12.0)
        return 0.0

    lane12 = lane_iota((12, 128))
    for x in range(12):
        cm = coef[x] * mu[x]
        for c in range(3):
            at = 16 * c + 3 + x // 2
            edge = (even if x % 2 == 0 else odd)[:, at : at + 1]
            extra = halo(c, x, 0, 12) + jnp.where(lane12 == 127, edge, 0.0)
            push = coef[x] * force[16 * x : 16 * x + 12, 128 * c : 128 * (c + 1)]
            fnext[c, x] = base[c, x] + cm * extra + push
    lane6 = lane_iota((6, 128))
    for x in range(6):
        cm = 0.25 * (ccoef[x] * cmu[x])
        for c in range(3):
            at = 16 * c + 3 + x
            extra = halo(c, x, 16, 6) + jnp.where(lane6 == 0, coarse_g[:, at : at + 1], 0.0)
            cnext[c, x] = cbase[c, x] + cm * extra


K = 24
PART = 80


def matrices(first, second):
    lanes = lane_iota((K, 128))
    base_lane = jnp.broadcast_to(64 + (first & 7), (K, 128))
    z = second & 127
    live = first >= 0
    here = jnp.where((lanes == z) & live, 1.0, 0.0)
    step = jnp.where((lanes == z + 1) & live, 1.0, 0.0) - jnp.where((lanes == z - 1) & live, 1.0, 0.0)
    lx = (second >> 11) - 1
    ly = ((second >> 7) & 15) - 1
    at = 16 * lx + ly
    place = lane_iota((K, 192))
    along_x = jnp.where(place == at + 16, 1.0, 0.0) - jnp.where(place == at - 16, 1.0, 0.0)
    along_y = jnp.where(place == at + 1, 1.0, 0.0) - jnp.where(place == at - 1, 1.0, 0.0)
    centre = jnp.where(place == at, 1.0, 0.0)
    part = [along_x, along_y, centre, jnp.zeros((8, 192), F32)]
    spread = jnp.concatenate(part * 3 + [jnp.zeros((256 - 3 * PART, 192), F32)], axis=0)
    pick = jnp.where(lane_iota((K, NX * NY)) == first >> 3, 1.0, 0.0)
    return pick, base_lane, here, step, spread.T.astype(jnp.bfloat16)


def columns(number, rank, first, second):
    want = (row_iota((K, 128)) + number * K).astype(F32)
    one = jnp.zeros((K, 128), F32)
    two = jnp.zeros((K, 128), F32)
    for r in range(32):
        same = rank[r : r + 1, :] == want
        one = one + jnp.where(same, first[r : r + 1, :], 0.0)
        two = two + jnp.where(same, second[r : r + 1, :], 0.0)
    one = jnp.sum(one, axis=1, keepdims=True).astype(jnp.int32) - 1
    two = jnp.sum(two, axis=1, keepdims=True).astype(jnp.int32)
    return one, two


def find_kernel(cells, pick, rank, first, second, base_lane, here, step, spread, hit_s):
    lane = lane_iota((1, 128))
    for r in range(32):
        part = cells[:, 128 * r : 128 * (r + 1)]
        lx = part[0:1, :] - 12 * lax.axis_index("gx")
        ly = part[1:2, :] - 12 * lax.axis_index("gy")
        inside = (lx >= -1) & (lx <= 12) & (ly >= -1) & (ly <= 12)
        hit_s[r : r + 1, :] = jnp.where(inside, 1.0, 0.0)
        first[r : r + 1, :] = (lane + (128 * r + 1)).astype(F32)
        second[r : r + 1, :] = (((lx + 1) << 11) + ((ly + 1) << 7) + part[2:3, :]).astype(F32)
    hit = hit_s[...]
    square = (128, 128)
    before = jnp.where(row_iota(square) < lane_iota(square), 1.0, 0.0)
    within = jnp.dot(hit, before, preferred_element_type=F32)
    total = jnp.dot(hit, jnp.ones(square, F32), preferred_element_type=F32)
    above = jnp.where(lane_iota((32, 32)) < row_iota((32, 32)), 1.0, 0.0)
    earlier = jnp.dot(above, total, preferred_element_type=F32)
    rank[...] = jnp.where(hit > 0.0, within + earlier, -1.0)
    one, two = columns(0, rank, first, second)
    pick[...], base_lane[...], here[...], step[...], spread[...] = matrices(one, two)


def exact_parts(x):
    parts = []
    for _ in range(3):
        parts.append(x.astype(jnp.bfloat16))
        x = x - parts[-1].astype(F32)
    return parts


def source_force(rows, pick, base_lane, here, step, spread):
    line = jnp.dot(
        pick.astype(jnp.bfloat16), jnp.concatenate(exact_parts(rows[...]), axis=1), preferred_element_type=F32
    )
    line = line[:, 0:128] + line[:, 128:256] + line[:, 256:384]
    lanes = lane_iota((K, 128)) - base_lane
    m = [0.5 * jnp.sum(jnp.where(lanes == 8 * i, line, 0.0), axis=1, keepdims=True) for i in range(6)]
    zeros = jnp.zeros((8, 128), F32)
    wide = []
    for a, b, c in ((0, 3, 4), (3, 1, 5), (4, 5, 2)):
        wide.append(jnp.concatenate([m[a] * here, m[b] * here, m[c] * step, zeros], axis=0))
    parts = exact_parts(jnp.concatenate(wide, axis=1))
    parts.append(jnp.zeros((256 - 3 * PART, 384), jnp.bfloat16))
    return jnp.dot(spread, jnp.concatenate(parts, axis=0), preferred_element_type=F32)


def shape(*dims):
    return jax.ShapeDtypeStruct(dims, F32)


def swapped(x, axis, first):
    pairs = [(i, i + 1) for i in range(first, lax.axis_size(axis) - 1, 2)]
    return lax.ppermute(x, axis, pairs + [(j, i) for i, j in pairs])


SMALL = pltpu.CompilerParams(vmem_limit_bytes=32 * 1024 * 1024)
PIECE = [VMEM((24, 128), F32), VMEM((16, 128), F32)]


def make_rows(fine_now, coarse_now, coarse_mu, src_moment):
    return pl.pallas_call(
        rows_kernel,
        in_specs=[pl.BlockSpec(memory_space=pltpu.HBM)] * 4,
        out_specs=vspec(1)[0],
        out_shape=shape(NX * NY, 128),
        scratch_shapes=PIECE
        + [
            VMEM((3, 12, 12, 128), F32),
            VMEM((3, 6, 6, 128), F32),
            VMEM((6, 6, 128), F32),
            VMEM((6, 8), F32),
            pltpu.SemaphoreType.DMA((6,)),
        ],
        compiler_params=pltpu.CompilerParams(vmem_limit_bytes=FIRST_LIMIT),
        name="make_rows",
    )(fine_now, coarse_now, coarse_mu, src_moment)


def pack_halos(fine_now, coarse_now, coarse_mu):
    return pl.pallas_call(
        pack_kernel,
        in_specs=vspec(3),
        out_specs=vspec(5),
        out_shape=[shape(16, 128)] + [shape(ROWS_X, 128)] * 2 + [shape(ROWS, 128)] * 2,
        scratch_shapes=PIECE,
        compiler_params=SMALL,
        name="pack_halos",
    )(fine_now, coarse_now, coarse_mu)


def find_sources(src_cell):
    return pl.pallas_call(
        find_kernel,
        in_specs=vspec(1),
        out_specs=vspec(8),
        out_shape=[
            shape(K, NX * NY),
            shape(32, 128), shape(32, 128), shape(32, 128),
            jax.ShapeDtypeStruct((K, 128), jnp.int32),
            shape(K, 128), shape(K, 128), jax.ShapeDtypeStruct((192, 256), jnp.bfloat16),
        ],
        scratch_shapes=[VMEM((32, 128), F32)],
        compiler_params=SMALL,
        name="find_sources",
    )(src_cell)


def base_step(*args):
    return pl.pallas_call(
        base_kernel,
        in_specs=vspec(10),
        out_specs=vspec(2),
        out_shape=[shape(3, 12, 12, 128), shape(3, 6, 6, 128)],
        scratch_shapes=[VMEM((36, 16, 128), F32), VMEM((18, 16, 128), F32)],
        compiler_params=SMALL,
        name="base_step",
    )(*args)


def finish(*args):
    return pl.pallas_call(
        finish_kernel,
        in_specs=vspec(20),
        out_specs=vspec(3),
        out_shape=[shape(3, 12, 12, 128), shape(3, 6, 6, 128), shape(3, 6, 6)],
        scratch_shapes=[
            VMEM((16, 128), F32),
            VMEM((16, 128), F32),
            VMEM((192, 384), F32),
        ],
        compiler_params=SMALL,
        name="finish",
    )(*args)


def local(
    fine_now, fine_prev, fine_mu, fine_coef, coarse_now, coarse_prev, coarse_mu, coarse_coef, src_cell, src_moment,
):
    rows = make_rows(fine_now, coarse_now, coarse_mu, src_moment)
    gathered = lax.all_to_all(rows.reshape(NX * NY, 1, 128), AX, 0, 0, tiled=True).reshape(NX * NY, 128)
    own, xa, xb, ya, yb = pack_halos(fine_now, coarse_now, coarse_mu)
    ya, yb = swapped(ya, "gy", 0), swapped(yb, "gy", 1)
    xb, xa = swapped(xb, "gx", 1), swapped(xa, "gx", 0)
    found = find_sources(src_cell)
    base = base_step(
        fine_now, fine_prev, fine_mu, fine_coef, coarse_now, coarse_prev, coarse_mu, coarse_coef, ya, yb
    )
    return finish(
        *found, *base, fine_mu, fine_coef, coarse_mu, coarse_coef, own, ya, yb, xb, xa, gathered
    )


def solution(mesh):
    in_specs = (
        P(None, "gx", "gy", None),
        P(None, "gx", "gy", None),
        P("gx", "gy", None),
        P("gx", "gy", None),
        P(None, "gx", "gy", None),
        P(None, "gx", "gy", None),
        P("gx", "gy", None),
        P("gx", "gy", None),
        P(),
        P(None, ("gx", "gy")),
    )
    out_specs = (P(None, "gx", "gy", None), P(None, "gx", "gy", None), P(None, "gx", "gy"))
    return jax.shard_map(local, mesh=mesh, in_specs=in_specs, out_specs=out_specs, check_vma=False)
```

time: 56 us -> 46.9 us (0.84)
  waiting for transfers between devices: 7.24 us -> 0.59 us
  local copies, waits for them, and re-layouts: 3.3 us -> 0.05 us
  starting transfers between devices: 38.1 us -> 39.8 us
  Pallas kernels: 6.07 us -> 5.31 us
    ppermute x4, waiting for transfers between devices: 7.24 us -> 0.59 us  [swapped(): return lax.ppermute(x, axis, pairs + [(j, i) for i, j in pairs])]
    unnamed x26 -> x18, local copies, waits for them, and re-layouts: 3.3 us -> 0.05 us
    ppermute x4, starting transfers between devices: 16.9 us -> 18.6 us  [swapped(): return lax.ppermute(x, axis, pairs + [(j, i) for i, j in pairs])]
    pallas_call x5, Pallas kernels: 6.07 us -> 5.31 us  [the longest x1 2.38 us: make_rows(): pl.pallas_call(rows_kernel, in_specs=[pl.BlockSpec(memory_space=pltpu.HBM...]
  transfers between devices with their start and end apart: 5 -> 5, of which waited for: 1 -> 1; matrix products, arithmetic and copies ran while one was open for 0% -> 0% of each run, Pallas kernels for 5% -> 3%
where the time goes in v2:
time: 46.9 us; the launch traced here: 46.6 us
  starting transfers between devices  39.8 us (85%)
  Pallas kernels  5.31 us (11%)
  between operations  0.85 us (2%)
  waiting for transfers between devices  0.59 us (1%)
    all_to_all x1, starting transfers between devices, local(): lax.all_to_all(rows.reshape(NX * NY, 1, 128), AX, 0, 0, tiled=True)  21.2 us
    ppermute x4, starting transfers between devices, swapped(): return lax.ppermute(x, axis, pairs + [(j, i) for i, j in pairs])  18.6 us
    pallas_call x1, Pallas kernels, make_rows(): pl.pallas_call(rows_kernel, in_specs=[pl.BlockSpec(memory_space=pltpu.HBM...  2.38 us
    pallas_call x1, Pallas kernels, finish(): pl.pallas_call(finish_kernel, in_specs=vspec(20), out_specs=vspec(3), out...  1.61 us
  transfers between devices with their start and end apart: 5, of which 1 were waited for; matrix products, arithmetic and copies ran while one was open for 0% of the time, Pallas kernels for 3%

profile of v2, /device:TPU:31, one launch (start us, length us, event | category | flops | bytes accessed | tf_op | source)
XLA Modules:
  0.0 46.6 jit_solution(13914347298327492410)
XLA Ops:
  0.6 2.4 %make_rows.1 = f32[512,128]{1,0:T(8,128)} custom-call(f32[3,12,12,128]{3,2,1,0:T(8,128)} %fine_hbm.1, f32[3,6,6,128]{3,2,1,0:T(8,128)} %coarse_hbm.1, f32[6,6,128]{2,1,0:T(8,128)} %cmu.3, f32[6,8]{1,0:T(8,128)} %mom_hbm.1), custom_call_target="tpu_custom_call" | custom-call | tf_op jit(solution)/shard_map/make_rows/pallas_call | solution.py:360
  3.0 0.0 copy-start
  3.0 0.0 copy-start.1
  3.1 0.0 copy-start.4
  3.1 0.0 copy-start.5
  3.1 21.2 %all-to-all-start = ((f32[512,1,128]{2,1,0:T(1,128)}), f32[512,1,128]{2,1,0:T(1,128)S(1)}, u32[]{:S(2)}, u32[]{:S(2)}) async-start(f32[512,1,128]{2,1,0:T(1,128)} %bitcast.5), calls=%async_computation | async-start | bytes 524288 | tf_op jit(solution)/shard_map/all_to_all | solution.py:439
  24.3 0.0 copy-done
  24.3 0.0 copy-start.2
  24.3 0.0 copy-start.3
  24.4 0.0 copy-start.7
  24.4 0.3 pack_halos.1
  24.7 3.6 %collective-permute-start = (f32[160,128]{1,0:T(8,128)S(1)}, f32[160,128]{1,0:T(8,128)S(1)}, u32[]{:S(2)}, u32[]{:S(2)}) collective-permute-start(f32[160,128]{1,0:T(8,128)S(1)} %get-tuple-element.26), channel_id=1, source_target_pairs={{0,1},{2,3},{4,5},{6,7},{8,9},{10,11},{12,13},{14,15},{1,0},{3,2},... | collective-permute-start | bytes 245768 | tf_op jit(solution)/shard_map/ppermute | solution.py:352
  28.3 7.3 %collective-permute-start.1 = (f32[160,128]{1,0:T(8,128)S(1)}, f32[160,128]{1,0:T(8,128)S(1)}, u32[]{:S(2)}, u32[]{:S(2)}) collective-permute-start(f32[160,128]{1,0:T(8,128)S(1)} %get-tuple-element.27), channel_id=1, source_target_pairs={{1,2},{3,4},{5,6},{7,8},{9,10},{11,12},{13,14},{2,1},{4,3},{6,5},{... | collective-permute-start | bytes 245768 | tf_op jit(solution)/shard_map/ppermute | solution.py:352
  35.6 5.7 %collective-permute-start.2 = (f32[160,128]{1,0:T(8,128)S(1)}, f32[160,128]{1,0:T(8,128)S(1)}, u32[]{:S(2)}, u32[]{:S(2)}) collective-permute-start(f32[160,128]{1,0:T(8,128)S(1)} %get-tuple-element.31), channel_id=1, source_target_pairs={{16,32},{48,64},{80,96},{112,128},{144,160},{176,192},{208,224},{2... | collective-permute-start | bytes 245768 | tf_op jit(solution)/shard_map/ppermute | solution.py:352
  41.3 0.0 copy-start.6
  41.4 1.9 %collective-permute-start.3 = (f32[160,128]{1,0:T(8,128)S(1)}, f32[160,128]{1,0:T(8,128)S(1)}, u32[]{:S(2)}, u32[]{:S(2)}) collective-permute-start(f32[160,128]{1,0:T(8,128)S(1)} %get-tuple-element.32), channel_id=1, source_target_pairs={{0,16},{32,48},{64,80},{96,112},{128,144},{160,176},{192,208},{224... | collective-permute-start | bytes 245768 | tf_op jit(solution)/shard_map/ppermute | solution.py:352
  43.3 0.6 %find_sources.1 = (f32[24,512]{1,0:T(8,128)S(1)}, f32[32,128]{1,0:T(8,128)S(1)}, f32[32,128]{1,0:T(8,128)S(1)}, f32[32,128]{1,0:T(8,128)S(1)}, s32[24,128]{1,0:T...) custom-call(s32[3,4096]{1,0:T(4,128)S(1)} %copy-done.8), custom_call_target="tpu_custom_call" | custom-call | tf_op jit(solution)/shard_map/find_sources/pallas_call | solution.py:391
  43.9 0.0 collective-permute-done.ya
  44.0 0.0 collective-permute-done.1.yb
  44.0 0.4 base_step.1
  44.4 0.6 %collective-permute-done.2.xb = f32[160,128]{1,0:T(8,128)S(1)} collective-permute-done((f32[160,128]{1,0:T(8,128)S(1)}, f32[160,128]{1,0:T(8,128)S(1)}, u32[]{:S(2)}, u32[]{:S(2)}) %collective-permute-start.2) | collective-permute-done | bytes 81952 | tf_op jit(solution)/shard_map/ppermute | solution.py:352
  45.0 0.0 collective-permute-done.3.xa
  45.0 0.0 all-to-all-done
  45.0 1.6 %finish.1 = (f32[3,12,12,128]{3,2,1,0:T(8,128)}, f32[3,6,6,128]{3,2,1,0:T(8,128)}, f32[3,6,6]{2,1,0:T(8,128)}) custom-call(f32[24,512]{1,0:T(8,128)S(1)} %get-tuple-element.18.pick, f32[32,128]{1,0:T(8,128)S(1)} %get-tuple-element.19.rank, f32[32,128]{1,0:T(8,128)S(1)} %get-tuple-element.20.first, f32[32,128]{1,0:T(8,128)S(1)} %get-tuple-element.21.second, ...), custom_call_target="tpu_custom_call" | custom-call | tf_op jit(solution)/shard_map/finish/pallas_call | solution.py:420
  (9 shorter events, 0.0 us)
Async XLA Ops:
  0.6 42.7 %copy-start.8 = (s32[3,4096]{1,0:T(4,128)S(1)}, s32[3,4096]{1,0:T(4,128)}, u32[]{:S(2)}) copy-start(s32[3,4096]{1,0:T(4,128)} %cells.1) | copy-start | bytes 147460
  3.0 21.3 %copy-start = (f32[3,12,12,128]{3,2,1,0:T(8,128)S(1)}, f32[3,12,12,128]{3,2,1,0:T(8,128)}, u32[]{:S(2)}) copy-start(f32[3,12,12,128]{3,2,1,0:T(8,128)} %fine_hbm.1) | copy-start | bytes 663556
  3.0 21.3 %copy-start.1 = (f32[3,6,6,128]{3,2,1,0:T(8,128)S(1)}, f32[3,6,6,128]{3,2,1,0:T(8,128)}, u32[]{:S(2)}) copy-start(f32[3,6,6,128]{3,2,1,0:T(8,128)} %coarse_hbm.1) | copy-start | bytes 165892
  3.1 21.3 %copy-start.4 = (f32[6,6,128]{2,1,0:T(8,128)S(1)}, f32[6,6,128]{2,1,0:T(8,128)}, u32[]{:S(2)}) copy-start(f32[6,6,128]{2,1,0:T(8,128)} %cmu.3) | copy-start | bytes 55300
  3.1 40.9 %copy-start.5 = (f32[3,12,12,128]{3,2,1,0:T(8,128)S(1)}, f32[3,12,12,128]{3,2,1,0:T(8,128)}, u32[]{:S(2)}) copy-start(f32[3,12,12,128]{3,2,1,0:T(8,128)} %prev.1) | copy-start | bytes 663556
  3.1 41.9 %all-to-all-start = ((f32[512,1,128]{2,1,0:T(1,128)}), f32[512,1,128]{2,1,0:T(1,128)S(1)}, u32[]{:S(2)}, u32[]{:S(2)}) async-start(f32[512,1,128]{2,1,0:T(1,128)} %bitcast.5), calls=%async_computation | async-start | bytes 524288 | tf_op jit(solution)/shard_map/all_to_all | solution.py:439
  24.3 19.6 %copy-start.2 = (f32[12,12,128]{2,1,0:T(8,128)S(1)}, f32[12,12,128]{2,1,0:T(8,128)}, u32[]{:S(2)}) copy-start(f32[12,12,128]{2,1,0:T(8,128)} %mu.5) | copy-start | bytes 221188
  24.3 19.6 %copy-start.3 = (f32[12,12,128]{2,1,0:T(8,128)S(1)}, f32[12,12,128]{2,1,0:T(8,128)}, u32[]{:S(2)}) copy-start(f32[12,12,128]{2,1,0:T(8,128)} %coef.3) | copy-start | bytes 221188
  24.4 19.6 %copy-start.7 = (f32[3,6,6,128]{3,2,1,0:T(8,128)S(1)}, f32[3,6,6,128]{3,2,1,0:T(8,128)}, u32[]{:S(2)}) copy-start(f32[3,6,6,128]{3,2,1,0:T(8,128)} %cprev.1) | copy-start | bytes 165892
  24.7 19.3 %collective-permute-start = (f32[160,128]{1,0:T(8,128)S(1)}, f32[160,128]{1,0:T(8,128)S(1)}, u32[]{:S(2)}, u32[]{:S(2)}) collective-permute-start(f32[160,128]{1,0:T(8,128)S(1)} %get-tuple-element.26), channel_id=1, source_target_pairs={{0,1},{2,3},{4,5},{6,7},{8,9},{10,11},{12,13},{14,15},{1,0},{3,2},... | collective-permute-start | bytes 245768 | tf_op jit(solution)/shard_map/ppermute | solution.py:352
  28.3 15.6 %collective-permute-start.1 = (f32[160,128]{1,0:T(8,128)S(1)}, f32[160,128]{1,0:T(8,128)S(1)}, u32[]{:S(2)}, u32[]{:S(2)}) collective-permute-start(f32[160,128]{1,0:T(8,128)S(1)} %get-tuple-element.27), channel_id=1, source_target_pairs={{1,2},{3,4},{5,6},{7,8},{9,10},{11,12},{13,14},{2,1},{4,3},{6,5},{... | collective-permute-start | bytes 245768 | tf_op jit(solution)/shard_map/ppermute | solution.py:352
  35.6 9.4 %collective-permute-start.2 = (f32[160,128]{1,0:T(8,128)S(1)}, f32[160,128]{1,0:T(8,128)S(1)}, u32[]{:S(2)}, u32[]{:S(2)}) collective-permute-start(f32[160,128]{1,0:T(8,128)S(1)} %get-tuple-element.31), channel_id=1, source_target_pairs={{16,32},{48,64},{80,96},{112,128},{144,160},{176,192},{208,224},{2... | collective-permute-start | bytes 245768 | tf_op jit(solution)/shard_map/ppermute | solution.py:352
  41.3 2.7 %copy-start.6 = (f32[6,6,128]{2,1,0:T(8,128)S(1)}, f32[6,6,128]{2,1,0:T(8,128)}, u32[]{:S(2)}) copy-start(f32[6,6,128]{2,1,0:T(8,128)} %ccoef.3) | copy-start | bytes 55300
  41.4 3.6 %collective-permute-start.3 = (f32[160,128]{1,0:T(8,128)S(1)}, f32[160,128]{1,0:T(8,128)S(1)}, u32[]{:S(2)}, u32[]{:S(2)}) collective-permute-start(f32[160,128]{1,0:T(8,128)S(1)} %get-tuple-element.32), channel_id=1, source_target_pairs={{0,16},{32,48},{64,80},{96,112},{128,144},{160,176},{192,208},{224... | collective-permute-start | bytes 245768 | tf_op jit(solution)/shard_map/ppermute | solution.py:352

commit v3 on v2

--- a/solution.py
+++ b/solution.py
@@ -9,10 +9,11 @@
 NX, NY = 32, 16
 FIRST_LIMIT = 60 * 1024 * 1024
 AX = ("gx", "gy")
-ROWS = 160
+ROWS_YA = 124
+ROWS_YB = 136
 GROW = 108
-ROWS_X = 160
-GROW_X = 144
+ROWS_XA = 120
+ROWS_XB = 128
 VMEM = pltpu.VMEM
 F32 = jnp.float32
 
@@ -108,9 +109,10 @@
 
     for c in range(3):
         for j in range(2):
-            at = 24 * (2 * c + j)
+            at = 12 * (2 * c + j)
             put((xa, xb), odd_x, slice(at, at + 12), fine[c, 10 + j], fine[c, j])
-            put((xa, xb), odd_x, slice(at + 16, at + 22), coarse[c, 4 + j], coarse[c, j])
+            at = 72 + 6 * (2 * c + j)
+            put((xa, xb), odd_x, slice(at, at + 6), coarse[c, 4 + j], coarse[c, j])
         for x in range(12):
             at = 2 * (12 * c + x)
             put((ya, yb), odd_y, slice(at, at + 2), fine[c, x, 10:12, :], fine[c, x, 0:2, :])
@@ -122,12 +124,13 @@
     here = slice(GROW, GROW + 16)
     up = jnp.where(place < 4, pltpu.roll(g, 128 - 6, 1), 0.0)
     down = jnp.where((place >= 9) & (place < 13), pltpu.roll(g, 6, 1), 0.0)
-    put((xa, xb), odd_x, slice(GROW_X, ROWS_X), up, down)
+    put((xa, xb), odd_x, slice(GROW, GROW + 8), up[3:11, :], down[3:11, :])
     up = jnp.where(row < 4, pltpu.roll(g, 16 - 6, 0), 0.0)
     down = jnp.where((row >= 9) & (row < 13), pltpu.roll(g, 6, 0), 0.0)
     put((ya, yb), odd_y, here, up, down)
-    for ref in (ya, yb):
-        ref[GROW + 16 : ROWS, :] = jnp.zeros((ROWS - GROW - 16, 128), F32)
+    xa[GROW + 8 : ROWS_XA, :] = jnp.zeros((ROWS_XA - GROW - 8, 128), F32)
+    yb[GROW + 16 : ROWS_YB, :] = jnp.zeros((ROWS_YB - GROW - 16, 128), F32)
+    xb[GROW + 8 : ROWS_XB, :] = jnp.zeros((ROWS_XB - GROW - 8, 128), F32)
 
 
 def inside(x, y):
@@ -186,9 +189,8 @@
     lane = lane_iota((16, 128))
     line = lane_iota((1, 128))
     force[...] = source_force(rows, pick[...], base_lane[...], here[...], step[...], spread[...])
-    g_s[...] = own[...]
-    for ref, at in ((ya, GROW), (yb, GROW), (xa, GROW_X), (xb, GROW_X)):
-        g_s[...] = g_s[...] + ref[at : at + 16, :]
+    g_s[...] = own[...] + ya[GROW : GROW + 16, :] + yb[GROW : GROW + 16, :]
+    g_s[3:11, :] = g_s[3:11, :] + xa[GROW : GROW + 8, :] + xb[GROW : GROW + 8, :]
     ix = lax.axis_index("gx")
     iy = lax.axis_index("gy")
     for a in (1, -1):
@@ -230,8 +232,9 @@
     odd_x = (ix & 1) == 1
 
     def halo(c, x, at, size):
-        low = [lower(slice(n + at, n + at + size), xa, xb, odd_x) for n in (48 * c, 48 * c + 24)]
-        high = [upper(slice(n + at, n + at + size), xa, xb, odd_x) for n in (48 * c, 48 * c + 24)]
+        rows = [slice(n, n + size) for n in (at + 2 * size * c, at + 2 * size * c + size)]
+        low = [lower(n, xa, xb, odd_x) for n in rows]
+        high = [upper(n, xa, xb, odd_x) for n in rows]
         if x == 0:
             return (16.0 * low[1] - low[0]) * (1.0 / 12.0)
         if x == 1:
@@ -256,7 +259,7 @@
         cm = 0.25 * (ccoef[x] * cmu[x])
         for c in range(3):
             at = 16 * c + 3 + x
-            extra = halo(c, x, 16, 6) + jnp.where(lane6 == 0, coarse_g[:, at : at + 1], 0.0)
+            extra = halo(c, x, 72, 6) + jnp.where(lane6 == 0, coarse_g[:, at : at + 1], 0.0)
             cnext[c, x] = cbase[c, x] + cm * extra
 
 
@@ -380,7 +383,7 @@
         pack_kernel,
         in_specs=vspec(3),
         out_specs=vspec(5),
-        out_shape=[shape(16, 128)] + [shape(ROWS_X, 128)] * 2 + [shape(ROWS, 128)] * 2,
+        out_shape=[shape(16, 128)] + [shape(n, 128) for n in (ROWS_XA, ROWS_XB, ROWS_YA, ROWS_YB)],
         scratch_shapes=PIECE,
         compiler_params=SMALL,
         name="pack_halos",

time: 46.9 us -> 45.9 us (0.979)
  starting transfers between devices: 39.8 us -> 38.9 us
    ppermute x4, starting transfers between devices: 18.6 us -> 17.7 us  [swapped(): return lax.ppermute(x, axis, pairs + [(j, i) for i, j in pairs])]
where the time goes in v3:
time: 45.9 us; the launch traced here: 45.6 us
  starting transfers between devices  38.9 us (85%)
  Pallas kernels  5.33 us (12%)
  between operations  0.85 us (2%)
  waiting for transfers between devices  0.49 us (1%)
    all_to_all x1, starting transfers between devices, local(): lax.all_to_all(rows.reshape(NX * NY, 1, 128), AX, 0, 0, tiled=True)  21.2 us
    ppermute x4, starting transfers between devices, swapped(): return lax.ppermute(x, axis, pairs + [(j, i) for i, j in pairs])  17.7 us
    pallas_call x1, Pallas kernels, make_rows(): pl.pallas_call(rows_kernel, in_specs=[pl.BlockSpec(memory_space=pltpu.HBM...  2.38 us
    pallas_call x1, Pallas kernels, finish(): pl.pallas_call(finish_kernel, in_specs=vspec(20), out_specs=vspec(3), out...  1.62 us
  transfers between devices with their start and end apart: 5, of which 1 were waited for; matrix products, arithmetic and copies ran while one was open for 0% of the time, Pallas kernels for 3%

profile of v3, /device:TPU:31, one launch (start us, length us, event | category | flops | bytes accessed | tf_op | source)
XLA Modules:
  0.0 45.6 jit_solution(5145748966049876313)
XLA Ops:
  0.6 2.4 %make_rows.1 = f32[512,128]{1,0:T(8,128)} custom-call(f32[3,12,12,128]{3,2,1,0:T(8,128)} %fine_hbm.1, f32[3,6,6,128]{3,2,1,0:T(8,128)} %coarse_hbm.1, f32[6,6,128]{2,1,0:T(8,128)} %cmu.3, f32[6,8]{1,0:T(8,128)} %mom_hbm.1), custom_call_target="tpu_custom_call" | custom-call | tf_op jit(solution)/shard_map/make_rows/pallas_call | solution.py:363
  3.0 0.0 copy-start
  3.0 0.0 copy-start.1
  3.1 0.0 copy-start.2
  3.1 0.0 copy-start.5
  3.1 21.2 %all-to-all-start = ((f32[512,1,128]{2,1,0:T(1,128)}), f32[512,1,128]{2,1,0:T(1,128)S(1)}, u32[]{:S(2)}, u32[]{:S(2)}) async-start(f32[512,1,128]{2,1,0:T(1,128)} %bitcast.5), calls=%async_computation | async-start | bytes 524288 | tf_op jit(solution)/shard_map/all_to_all | solution.py:442
  24.3 0.0 copy-start.3
  24.3 0.0 copy-start.4
  24.4 0.0 copy-start.7
  24.4 0.3 pack_halos.1
  24.7 8.3 %collective-permute-start.1 = (f32[136,128]{1,0:T(8,128)S(1)}, f32[136,128]{1,0:T(8,128)S(1)}, u32[]{:S(2)}, u32[]{:S(2)}) collective-permute-start(f32[136,128]{1,0:T(8,128)S(1)} %get-tuple-element.27), channel_id=1, source_target_pairs={{1,2},{3,4},{5,6},{7,8},{9,10},{11,12},{13,14},{2,1},{4,3},{6,5},{... | collective-permute-start | bytes 208904 | tf_op jit(solution)/shard_map/ppermute | solution.py:355
  33.0 5.5 %collective-permute-start.2 = (f32[128,128]{1,0:T(8,128)S(1)}, f32[128,128]{1,0:T(8,128)S(1)}, u32[]{:S(2)}, u32[]{:S(2)}) collective-permute-start(f32[128,128]{1,0:T(8,128)S(1)} %get-tuple-element.31), channel_id=1, source_target_pairs={{16,32},{48,64},{80,96},{112,128},{144,160},{176,192},{208,224},{2... | collective-permute-start | bytes 196616 | tf_op jit(solution)/shard_map/ppermute | solution.py:355
  38.5 1.9 %collective-permute-start = (f32[124,128]{1,0:T(8,128)S(1)}, f32[124,128]{1,0:T(8,128)S(1)}, u32[]{:S(2)}, u32[]{:S(2)}) collective-permute-start(f32[124,128]{1,0:T(8,128)S(1)} %get-tuple-element.26), channel_id=1, source_target_pairs={{0,1},{2,3},{4,5},{6,7},{8,9},{10,11},{12,13},{14,15},{1,0},{3,2},... | collective-permute-start | bytes 190472 | tf_op jit(solution)/shard_map/ppermute | solution.py:355
  40.4 0.0 copy-start.6
  40.4 1.9 %collective-permute-start.3 = (f32[120,128]{1,0:T(8,128)S(1)}, f32[120,128]{1,0:T(8,128)S(1)}, u32[]{:S(2)}, u32[]{:S(2)}) collective-permute-start(f32[120,128]{1,0:T(8,128)S(1)} %get-tuple-element.32), channel_id=1, source_target_pairs={{0,16},{32,48},{64,80},{96,112},{128,144},{160,176},{192,208},{224... | collective-permute-start | bytes 184328 | tf_op jit(solution)/shard_map/ppermute | solution.py:355
  42.4 0.0 copy-done.8
  42.4 0.6 %find_sources.1 = (f32[24,512]{1,0:T(8,128)S(1)}, f32[32,128]{1,0:T(8,128)S(1)}, f32[32,128]{1,0:T(8,128)S(1)}, f32[32,128]{1,0:T(8,128)S(1)}, s32[24,128]{1,0:T...) custom-call(s32[3,4096]{1,0:T(4,128)S(1)} %copy-done.8), custom_call_target="tpu_custom_call" | custom-call | tf_op jit(solution)/shard_map/find_sources/pallas_call | solution.py:394
  43.0 0.5 %collective-permute-done.ya = f32[124,128]{1,0:T(8,128)S(1)} collective-permute-done((f32[124,128]{1,0:T(8,128)S(1)}, f32[124,128]{1,0:T(8,128)S(1)}, u32[]{:S(2)}, u32[]{:S(2)}) %collective-permute-start) | collective-permute-done | bytes 63520 | tf_op jit(solution)/shard_map/ppermute | solution.py:355
  43.5 0.0 collective-permute-done.1.yb
  43.6 0.4 base_step.1
  43.9 0.0 collective-permute-done.3.xa
  44.0 0.0 collective-permute-done.2.xb
  44.0 0.0 all-to-all-done
  44.0 1.6 %finish.1 = (f32[3,12,12,128]{3,2,1,0:T(8,128)}, f32[3,6,6,128]{3,2,1,0:T(8,128)}, f32[3,6,6]{2,1,0:T(8,128)}) custom-call(f32[24,512]{1,0:T(8,128)S(1)} %get-tuple-element.18.pick, f32[32,128]{1,0:T(8,128)S(1)} %get-tuple-element.19.rank, f32[32,128]{1,0:T(8,128)S(1)} %get-tuple-element.20.first, f32[32,128]{1,0:T(8,128)S(1)} %get-tuple-element.21.second, ...), custom_call_target="tpu_custom_call" | custom-call | tf_op jit(solution)/shard_map/finish/pallas_call | solution.py:423
  (9 shorter events, 0.0 us)
Async XLA Ops:
  0.6 41.7 %copy-start.8 = (s32[3,4096]{1,0:T(4,128)S(1)}, s32[3,4096]{1,0:T(4,128)}, u32[]{:S(2)}) copy-start(s32[3,4096]{1,0:T(4,128)} %cells.1) | copy-start | bytes 147460
  3.0 21.3 %copy-start = (f32[3,12,12,128]{3,2,1,0:T(8,128)S(1)}, f32[3,12,12,128]{3,2,1,0:T(8,128)}, u32[]{:S(2)}) copy-start(f32[3,12,12,128]{3,2,1,0:T(8,128)} %fine_hbm.1) | copy-start | bytes 663556
  3.0 21.3 %copy-start.1 = (f32[3,6,6,128]{3,2,1,0:T(8,128)S(1)}, f32[3,6,6,128]{3,2,1,0:T(8,128)}, u32[]{:S(2)}) copy-start(f32[3,6,6,128]{3,2,1,0:T(8,128)} %coarse_hbm.1) | copy-start | bytes 165892
  3.1 21.3 %copy-start.2 = (f32[6,6,128]{2,1,0:T(8,128)S(1)}, f32[6,6,128]{2,1,0:T(8,128)}, u32[]{:S(2)}) copy-start(f32[6,6,128]{2,1,0:T(8,128)} %cmu.3) | copy-start | bytes 55300
  3.1 40.5 %copy-start.5 = (f32[3,12,12,128]{3,2,1,0:T(8,128)S(1)}, f32[3,12,12,128]{3,2,1,0:T(8,128)}, u32[]{:S(2)}) copy-start(f32[3,12,12,128]{3,2,1,0:T(8,128)} %prev.1) | copy-start | bytes 663556
  3.1 40.9 %all-to-all-start = ((f32[512,1,128]{2,1,0:T(1,128)}), f32[512,1,128]{2,1,0:T(1,128)S(1)}, u32[]{:S(2)}, u32[]{:S(2)}) async-start(f32[512,1,128]{2,1,0:T(1,128)} %bitcast.5), calls=%async_computation | async-start | bytes 524288 | tf_op jit(solution)/shard_map/all_to_all | solution.py:442
  24.3 19.2 %copy-start.3 = (f32[12,12,128]{2,1,0:T(8,128)S(1)}, f32[12,12,128]{2,1,0:T(8,128)}, u32[]{:S(2)}) copy-start(f32[12,12,128]{2,1,0:T(8,128)} %mu.5) | copy-start | bytes 221188
  24.3 19.2 %copy-start.4 = (f32[12,12,128]{2,1,0:T(8,128)S(1)}, f32[12,12,128]{2,1,0:T(8,128)}, u32[]{:S(2)}) copy-start(f32[12,12,128]{2,1,0:T(8,128)} %coef.3) | copy-start | bytes 221188
  24.4 19.2 %copy-start.7 = (f32[3,6,6,128]{3,2,1,0:T(8,128)S(1)}, f32[3,6,6,128]{3,2,1,0:T(8,128)}, u32[]{:S(2)}) copy-start(f32[3,6,6,128]{3,2,1,0:T(8,128)} %cprev.1) | copy-start | bytes 165892
  24.7 18.8 %collective-permute-start.1 = (f32[136,128]{1,0:T(8,128)S(1)}, f32[136,128]{1,0:T(8,128)S(1)}, u32[]{:S(2)}, u32[]{:S(2)}) collective-permute-start(f32[136,128]{1,0:T(8,128)S(1)} %get-tuple-element.27), channel_id=1, source_target_pairs={{1,2},{3,4},{5,6},{7,8},{9,10},{11,12},{13,14},{2,1},{4,3},{6,5},{... | collective-permute-start | bytes 208904 | tf_op jit(solution)/shard_map/ppermute | solution.py:355
  33.0 10.9 %collective-permute-start.2 = (f32[128,128]{1,0:T(8,128)S(1)}, f32[128,128]{1,0:T(8,128)S(1)}, u32[]{:S(2)}, u32[]{:S(2)}) collective-permute-start(f32[128,128]{1,0:T(8,128)S(1)} %get-tuple-element.31), channel_id=1, source_target_pairs={{16,32},{48,64},{80,96},{112,128},{144,160},{176,192},{208,224},{2... | collective-permute-start | bytes 196616 | tf_op jit(solution)/shard_map/ppermute | solution.py:355
  38.5 5.0 %collective-permute-start = (f32[124,128]{1,0:T(8,128)S(1)}, f32[124,128]{1,0:T(8,128)S(1)}, u32[]{:S(2)}, u32[]{:S(2)}) collective-permute-start(f32[124,128]{1,0:T(8,128)S(1)} %get-tuple-element.26), channel_id=1, source_target_pairs={{0,1},{2,3},{4,5},{6,7},{8,9},{10,11},{12,13},{14,15},{1,0},{3,2},... | collective-permute-start | bytes 190472 | tf_op jit(solution)/shard_map/ppermute | solution.py:355
  40.4 3.1 %copy-start.6 = (f32[6,6,128]{2,1,0:T(8,128)S(1)}, f32[6,6,128]{2,1,0:T(8,128)}, u32[]{:S(2)}) copy-start(f32[6,6,128]{2,1,0:T(8,128)} %ccoef.3) | copy-start | bytes 55300
  40.4 3.5 %collective-permute-start.3 = (f32[120,128]{1,0:T(8,128)S(1)}, f32[120,128]{1,0:T(8,128)S(1)}, u32[]{:S(2)}, u32[]{:S(2)}) collective-permute-start(f32[120,128]{1,0:T(8,128)S(1)} %get-tuple-element.32), channel_id=1, source_target_pairs={{0,16},{32,48},{64,80},{96,112},{128,144},{160,176},{192,208},{224... | collective-permute-start | bytes 184328 | tf_op jit(solution)/shard_map/ppermute | solution.py:355

commit v4 on v3

--- a/solution.py
+++ b/solution.py
@@ -300,17 +300,16 @@
     return one, two
 
 
-def find_kernel(cells, pick, rank, first, second, base_lane, here, step, spread, hit_s):
-    lane = lane_iota((1, 128))
+def find_kernel(cells, pick, rank, first, second, base_lane, here, step, spread, cell_s):
     for r in range(32):
-        part = cells[:, 128 * r : 128 * (r + 1)]
-        lx = part[0:1, :] - 12 * lax.axis_index("gx")
-        ly = part[1:2, :] - 12 * lax.axis_index("gy")
-        inside = (lx >= -1) & (lx <= 12) & (ly >= -1) & (ly <= 12)
-        hit_s[r : r + 1, :] = jnp.where(inside, 1.0, 0.0)
-        first[r : r + 1, :] = (lane + (128 * r + 1)).astype(F32)
-        second[r : r + 1, :] = (((lx + 1) << 11) + ((ly + 1) << 7) + part[2:3, :]).astype(F32)
-    hit = hit_s[...]
+        for n in range(3):
+            cell_s[n, r : r + 1, :] = cells[n : n + 1, 128 * r : 128 * (r + 1)]
+    lx = cell_s[0] - 12 * lax.axis_index("gx")
+    ly = cell_s[1] - 12 * lax.axis_index("gy")
+    hit = jnp.where((lx >= -1) & (lx <= 12) & (ly >= -1) & (ly <= 12), 1.0, 0.0)
+    block = (32, 128)
+    first[...] = (lane_iota(block) + 128 * row_iota(block) + 1).astype(F32)
+    second[...] = (((lx + 1) << 11) + ((ly + 1) << 7) + cell_s[2]).astype(F32)
     square = (128, 128)
     before = jnp.where(row_iota(square) < lane_iota(square), 1.0, 0.0)
     within = jnp.dot(hit, before, preferred_element_type=F32)
@@ -401,7 +400,7 @@
             jax.ShapeDtypeStruct((K, 128), jnp.int32),
             shape(K, 128), shape(K, 128), jax.ShapeDtypeStruct((192, 256), jnp.bfloat16),
         ],
-        scratch_shapes=[VMEM((32, 128), F32)],
+        scratch_shapes=[VMEM((3, 32, 128), jnp.int32)],
         compiler_params=SMALL,
         name="find_sources",
     )(src_cell)

time: 45.9 us -> 45.9 us (level)
  no operation moved by 1% of the time
where the time goes in v4:
time: 45.9 us; the launch traced here: 45.6 us
  starting transfers between devices  38.9 us (85%)
  Pallas kernels  5.26 us (11%)
  between operations  0.85 us (2%)
  waiting for transfers between devices  0.57 us (1%)
    all_to_all x1, starting transfers between devices, local(): lax.all_to_all(rows.reshape(NX * NY, 1, 128), AX, 0, 0, tiled=True)  21.2 us
    ppermute x4, starting transfers between devices, swapped(): return lax.ppermute(x, axis, pairs + [(j, i) for i, j in pairs])  17.7 us
    pallas_call x1, Pallas kernels, make_rows(): pl.pallas_call(rows_kernel, in_specs=[pl.BlockSpec(memory_space=pltpu.HBM...  2.38 us
    pallas_call x1, Pallas kernels, finish(): pl.pallas_call(finish_kernel, in_specs=vspec(20), out_specs=vspec(3), out...  1.62 us
  transfers between devices with their start and end apart: 5, of which 1 were waited for; matrix products, arithmetic and copies ran while one was open for 0% of the time, Pallas kernels for 3%

profile of v4, /device:TPU:31, one launch (start us, length us, event | category | flops | bytes accessed | tf_op | source)
XLA Modules:
  0.0 45.6 jit_solution(16717220157656724211)
XLA Ops:
  0.6 0.0 copy-start.8
  0.6 2.4 %make_rows.1 = f32[512,128]{1,0:T(8,128)} custom-call(f32[3,12,12,128]{3,2,1,0:T(8,128)} %fine_hbm.1, f32[3,6,6,128]{3,2,1,0:T(8,128)} %coarse_hbm.1, f32[6,6,128]{2,1,0:T(8,128)} %cmu.3, f32[6,8]{1,0:T(8,128)} %mom_hbm.1), custom_call_target="tpu_custom_call" | custom-call | tf_op jit(solution)/shard_map/make_rows/pallas_call | solution.py:362
  3.0 0.0 copy-start
  3.0 0.0 copy-start.1
  3.1 0.0 copy-start.2
  3.1 0.0 copy-start.5
  3.1 21.2 %all-to-all-start = ((f32[512,1,128]{2,1,0:T(1,128)}), f32[512,1,128]{2,1,0:T(1,128)S(1)}, u32[]{:S(2)}, u32[]{:S(2)}) async-start(f32[512,1,128]{2,1,0:T(1,128)} %bitcast.5), calls=%async_computation | async-start | bytes 524288 | tf_op jit(solution)/shard_map/all_to_all | solution.py:441
  24.3 0.0 copy-start.3
  24.3 0.0 copy-start.4
  24.4 0.0 copy-start.7
  24.4 0.3 pack_halos.1
  24.7 8.3 %collective-permute-start.1 = (f32[136,128]{1,0:T(8,128)S(1)}, f32[136,128]{1,0:T(8,128)S(1)}, u32[]{:S(2)}, u32[]{:S(2)}) collective-permute-start(f32[136,128]{1,0:T(8,128)S(1)} %get-tuple-element.27), channel_id=1, source_target_pairs={{1,2},{3,4},{5,6},{7,8},{9,10},{11,12},{13,14},{2,1},{4,3},{6,5},{... | collective-permute-start | bytes 208904 | tf_op jit(solution)/shard_map/ppermute | solution.py:354
  33.0 5.5 %collective-permute-start.2 = (f32[128,128]{1,0:T(8,128)S(1)}, f32[128,128]{1,0:T(8,128)S(1)}, u32[]{:S(2)}, u32[]{:S(2)}) collective-permute-start(f32[128,128]{1,0:T(8,128)S(1)} %get-tuple-element.31), channel_id=1, source_target_pairs={{16,32},{48,64},{80,96},{112,128},{144,160},{176,192},{208,224},{2... | collective-permute-start | bytes 196616 | tf_op jit(solution)/shard_map/ppermute | solution.py:354
  38.5 1.9 %collective-permute-start = (f32[124,128]{1,0:T(8,128)S(1)}, f32[124,128]{1,0:T(8,128)S(1)}, u32[]{:S(2)}, u32[]{:S(2)}) collective-permute-start(f32[124,128]{1,0:T(8,128)S(1)} %get-tuple-element.26), channel_id=1, source_target_pairs={{0,1},{2,3},{4,5},{6,7},{8,9},{10,11},{12,13},{14,15},{1,0},{3,2},... | collective-permute-start | bytes 190472 | tf_op jit(solution)/shard_map/ppermute | solution.py:354
  40.4 0.0 copy-start.6
  40.4 1.9 %collective-permute-start.3 = (f32[120,128]{1,0:T(8,128)S(1)}, f32[120,128]{1,0:T(8,128)S(1)}, u32[]{:S(2)}, u32[]{:S(2)}) collective-permute-start(f32[120,128]{1,0:T(8,128)S(1)} %get-tuple-element.32), channel_id=1, source_target_pairs={{0,16},{32,48},{64,80},{96,112},{128,144},{160,176},{192,208},{224... | collective-permute-start | bytes 184328 | tf_op jit(solution)/shard_map/ppermute | solution.py:354
  42.4 0.6 %find_sources.1 = (f32[24,512]{1,0:T(8,128)S(1)}, f32[32,128]{1,0:T(8,128)S(1)}, f32[32,128]{1,0:T(8,128)S(1)}, f32[32,128]{1,0:T(8,128)S(1)}, s32[24,128]{1,0:T...) custom-call(s32[3,4096]{1,0:T(4,128)S(1)} %copy-done.8), custom_call_target="tpu_custom_call" | custom-call | tf_op jit(solution)/shard_map/find_sources/pallas_call | solution.py:393
  43.0 0.6 %collective-permute-done.ya = f32[124,128]{1,0:T(8,128)S(1)} collective-permute-done((f32[124,128]{1,0:T(8,128)S(1)}, f32[124,128]{1,0:T(8,128)S(1)}, u32[]{:S(2)}, u32[]{:S(2)}) %collective-permute-start) | collective-permute-done | bytes 63520 | tf_op jit(solution)/shard_map/ppermute | solution.py:354
  43.5 0.0 collective-permute-done.1.yb
  43.6 0.4 base_step.1
  43.9 0.0 collective-permute-done.3.xa
  44.0 0.0 collective-permute-done.2.xb
  44.0 0.0 all-to-all-done
  44.0 1.6 %finish.1 = (f32[3,12,12,128]{3,2,1,0:T(8,128)}, f32[3,6,6,128]{3,2,1,0:T(8,128)}, f32[3,6,6]{2,1,0:T(8,128)}) custom-call(f32[24,512]{1,0:T(8,128)S(1)} %get-tuple-element.18.pick, f32[32,128]{1,0:T(8,128)S(1)} %get-tuple-element.19.rank, f32[32,128]{1,0:T(8,128)S(1)} %get-tuple-element.20.first, f32[32,128]{1,0:T(8,128)S(1)} %get-tuple-element.21.second, ...), custom_call_target="tpu_custom_call" | custom-call | tf_op jit(solution)/shard_map/finish/pallas_call | solution.py:422
  (9 shorter events, 0.0 us)
Async XLA Ops:
  0.6 41.7 %copy-start.8 = (s32[3,4096]{1,0:T(4,128)S(1)}, s32[3,4096]{1,0:T(4,128)}, u32[]{:S(2)}) copy-start(s32[3,4096]{1,0:T(4,128)} %cells.1) | copy-start | bytes 147460
  3.0 21.3 %copy-start = (f32[3,12,12,128]{3,2,1,0:T(8,128)S(1)}, f32[3,12,12,128]{3,2,1,0:T(8,128)}, u32[]{:S(2)}) copy-start(f32[3,12,12,128]{3,2,1,0:T(8,128)} %fine_hbm.1) | copy-start | bytes 663556
  3.0 21.3 %copy-start.1 = (f32[3,6,6,128]{3,2,1,0:T(8,128)S(1)}, f32[3,6,6,128]{3,2,1,0:T(8,128)}, u32[]{:S(2)}) copy-start(f32[3,6,6,128]{3,2,1,0:T(8,128)} %coarse_hbm.1) | copy-start | bytes 165892
  3.1 21.3 %copy-start.2 = (f32[6,6,128]{2,1,0:T(8,128)S(1)}, f32[6,6,128]{2,1,0:T(8,128)}, u32[]{:S(2)}) copy-start(f32[6,6,128]{2,1,0:T(8,128)} %cmu.3) | copy-start | bytes 55300
  3.1 40.5 %copy-start.5 = (f32[3,12,12,128]{3,2,1,0:T(8,128)S(1)}, f32[3,12,12,128]{3,2,1,0:T(8,128)}, u32[]{:S(2)}) copy-start(f32[3,12,12,128]{3,2,1,0:T(8,128)} %prev.1) | copy-start | bytes 663556
  3.1 40.9 %all-to-all-start = ((f32[512,1,128]{2,1,0:T(1,128)}), f32[512,1,128]{2,1,0:T(1,128)S(1)}, u32[]{:S(2)}, u32[]{:S(2)}) async-start(f32[512,1,128]{2,1,0:T(1,128)} %bitcast.5), calls=%async_computation | async-start | bytes 524288 | tf_op jit(solution)/shard_map/all_to_all | solution.py:441
  24.3 19.2 %copy-start.3 = (f32[12,12,128]{2,1,0:T(8,128)S(1)}, f32[12,12,128]{2,1,0:T(8,128)}, u32[]{:S(2)}) copy-start(f32[12,12,128]{2,1,0:T(8,128)} %mu.5) | copy-start | bytes 221188
  24.3 19.2 %copy-start.4 = (f32[12,12,128]{2,1,0:T(8,128)S(1)}, f32[12,12,128]{2,1,0:T(8,128)}, u32[]{:S(2)}) copy-start(f32[12,12,128]{2,1,0:T(8,128)} %coef.3) | copy-start | bytes 221188
  24.4 19.2 %copy-start.7 = (f32[3,6,6,128]{3,2,1,0:T(8,128)S(1)}, f32[3,6,6,128]{3,2,1,0:T(8,128)}, u32[]{:S(2)}) copy-start(f32[3,6,6,128]{3,2,1,0:T(8,128)} %cprev.1) | copy-start | bytes 165892
  24.7 18.8 %collective-permute-start.1 = (f32[136,128]{1,0:T(8,128)S(1)}, f32[136,128]{1,0:T(8,128)S(1)}, u32[]{:S(2)}, u32[]{:S(2)}) collective-permute-start(f32[136,128]{1,0:T(8,128)S(1)} %get-tuple-element.27), channel_id=1, source_target_pairs={{1,2},{3,4},{5,6},{7,8},{9,10},{11,12},{13,14},{2,1},{4,3},{6,5},{... | collective-permute-start | bytes 208904 | tf_op jit(solution)/shard_map/ppermute | solution.py:354
  33.0 10.9 %collective-permute-start.2 = (f32[128,128]{1,0:T(8,128)S(1)}, f32[128,128]{1,0:T(8,128)S(1)}, u32[]{:S(2)}, u32[]{:S(2)}) collective-permute-start(f32[128,128]{1,0:T(8,128)S(1)} %get-tuple-element.31), channel_id=1, source_target_pairs={{16,32},{48,64},{80,96},{112,128},{144,160},{176,192},{208,224},{2... | collective-permute-start | bytes 196616 | tf_op jit(solution)/shard_map/ppermute | solution.py:354
  38.5 5.0 %collective-permute-start = (f32[124,128]{1,0:T(8,128)S(1)}, f32[124,128]{1,0:T(8,128)S(1)}, u32[]{:S(2)}, u32[]{:S(2)}) collective-permute-start(f32[124,128]{1,0:T(8,128)S(1)} %get-tuple-element.26), channel_id=1, source_target_pairs={{0,1},{2,3},{4,5},{6,7},{8,9},{10,11},{12,13},{14,15},{1,0},{3,2},... | collective-permute-start | bytes 190472 | tf_op jit(solution)/shard_map/ppermute | solution.py:354
  40.4 3.1 %copy-start.6 = (f32[6,6,128]{2,1,0:T(8,128)S(1)}, f32[6,6,128]{2,1,0:T(8,128)}, u32[]{:S(2)}) copy-start(f32[6,6,128]{2,1,0:T(8,128)} %ccoef.3) | copy-start | bytes 55300
  40.4 3.5 %collective-permute-start.3 = (f32[120,128]{1,0:T(8,128)S(1)}, f32[120,128]{1,0:T(8,128)S(1)}, u32[]{:S(2)}, u32[]{:S(2)}) collective-permute-start(f32[120,128]{1,0:T(8,128)S(1)} %get-tuple-element.32), channel_id=1, source_target_pairs={{0,16},{32,48},{64,80},{96,112},{128,144},{160,176},{192,208},{224... | collective-permute-start | bytes 184328 | tf_op jit(solution)/shard_map/ppermute | solution.py:354

commit v5 on v4

--- a/solution.py
+++ b/solution.py
@@ -68,7 +68,7 @@
     copies.append(pltpu.make_async_copy(coarse_hbm, coarse, sems.at[3]))
     copies.append(pltpu.make_async_copy(mu_hbm, mu, sems.at[4]))
     copies.append(pltpu.make_async_copy(mom_hbm, mom, sems.at[5]))
-    for n in (5, 3, 4, 0, 1, 2):
+    for n in (0, 1, 2, 5, 3, 4):
         copies[n].start()
     lane = lane_iota((1, 128))
     lanes = lane_iota((6, 128))

time: 45.9 us -> 46 us (level)
  no operation moved by 1% of the time
where the time goes in v5:
time: 46 us; the launch traced here: 45.7 us
  starting transfers between devices  38.9 us (85%)
  Pallas kernels  5.37 us (12%)
  between operations  0.85 us (2%)
  waiting for transfers between devices  0.57 us (1%)
    all_to_all x1, starting transfers between devices, local(): lax.all_to_all(rows.reshape(NX * NY, 1, 128), AX, 0, 0, tiled=True)  21.2 us
    ppermute x4, starting transfers between devices, swapped(): return lax.ppermute(x, axis, pairs + [(j, i) for i, j in pairs])  17.7 us
    pallas_call x1, Pallas kernels, make_rows(): pl.pallas_call(rows_kernel, in_specs=[pl.BlockSpec(memory_space=pltpu.HBM...  2.49 us
    pallas_call x1, Pallas kernels, finish(): pl.pallas_call(finish_kernel, in_specs=vspec(20), out_specs=vspec(3), out...  1.62 us
  transfers between devices with their start and end apart: 5, of which 1 were waited for; matrix products, arithmetic and copies ran while one was open for 0% of the time, Pallas kernels for 3%

profile of v5, /device:TPU:31, one launch (start us, length us, event | category | flops | bytes accessed | tf_op | source)
XLA Modules:
  0.0 45.7 jit_solution(14781107209778161295)
XLA Ops:
  0.6 0.0 copy-start.8
  0.6 2.5 %make_rows.1 = f32[512,128]{1,0:T(8,128)} custom-call(f32[3,12,12,128]{3,2,1,0:T(8,128)} %fine_hbm.1, f32[3,6,6,128]{3,2,1,0:T(8,128)} %coarse_hbm.1, f32[6,6,128]{2,1,0:T(8,128)} %cmu.3, f32[6,8]{1,0:T(8,128)} %mom_hbm.1), custom_call_target="tpu_custom_call" | custom-call | tf_op jit(solution)/shard_map/make_rows/pallas_call | solution.py:362
  3.1 0.0 copy-start
  3.2 0.0 copy-start.1
  3.2 0.0 copy-start.2
  3.2 0.0 copy-start.5
  3.2 21.2 %all-to-all-start = ((f32[512,1,128]{2,1,0:T(1,128)}), f32[512,1,128]{2,1,0:T(1,128)S(1)}, u32[]{:S(2)}, u32[]{:S(2)}) async-start(f32[512,1,128]{2,1,0:T(1,128)} %bitcast.5), calls=%async_computation | async-start | bytes 524288 | tf_op jit(solution)/shard_map/all_to_all | solution.py:441
  24.4 0.0 copy-start.3
  24.5 0.0 copy-start.4
  24.5 0.0 copy-start.7
  24.5 0.3 pack_halos.1
  24.8 8.3 %collective-permute-start.1 = (f32[136,128]{1,0:T(8,128)S(1)}, f32[136,128]{1,0:T(8,128)S(1)}, u32[]{:S(2)}, u32[]{:S(2)}) collective-permute-start(f32[136,128]{1,0:T(8,128)S(1)} %get-tuple-element.27), channel_id=1, source_target_pairs={{1,2},{3,4},{5,6},{7,8},{9,10},{11,12},{13,14},{2,1},{4,3},{6,5},{... | collective-permute-start | bytes 208904 | tf_op jit(solution)/shard_map/ppermute | solution.py:354
  33.1 5.5 %collective-permute-start.2 = (f32[128,128]{1,0:T(8,128)S(1)}, f32[128,128]{1,0:T(8,128)S(1)}, u32[]{:S(2)}, u32[]{:S(2)}) collective-permute-start(f32[128,128]{1,0:T(8,128)S(1)} %get-tuple-element.31), channel_id=1, source_target_pairs={{16,32},{48,64},{80,96},{112,128},{144,160},{176,192},{208,224},{2... | collective-permute-start | bytes 196616 | tf_op jit(solution)/shard_map/ppermute | solution.py:354
  38.6 1.9 %collective-permute-start = (f32[124,128]{1,0:T(8,128)S(1)}, f32[124,128]{1,0:T(8,128)S(1)}, u32[]{:S(2)}, u32[]{:S(2)}) collective-permute-start(f32[124,128]{1,0:T(8,128)S(1)} %get-tuple-element.26), channel_id=1, source_target_pairs={{0,1},{2,3},{4,5},{6,7},{8,9},{10,11},{12,13},{14,15},{1,0},{3,2},... | collective-permute-start | bytes 190472 | tf_op jit(solution)/shard_map/ppermute | solution.py:354
  40.5 0.0 copy-start.6
  40.6 1.9 %collective-permute-start.3 = (f32[120,128]{1,0:T(8,128)S(1)}, f32[120,128]{1,0:T(8,128)S(1)}, u32[]{:S(2)}, u32[]{:S(2)}) collective-permute-start(f32[120,128]{1,0:T(8,128)S(1)} %get-tuple-element.32), channel_id=1, source_target_pairs={{0,16},{32,48},{64,80},{96,112},{128,144},{160,176},{192,208},{224... | collective-permute-start | bytes 184328 | tf_op jit(solution)/shard_map/ppermute | solution.py:354
  42.5 0.6 %find_sources.1 = (f32[24,512]{1,0:T(8,128)S(1)}, f32[32,128]{1,0:T(8,128)S(1)}, f32[32,128]{1,0:T(8,128)S(1)}, f32[32,128]{1,0:T(8,128)S(1)}, s32[24,128]{1,0:T...) custom-call(s32[3,4096]{1,0:T(4,128)S(1)} %copy-done.8), custom_call_target="tpu_custom_call" | custom-call | tf_op jit(solution)/shard_map/find_sources/pallas_call | solution.py:393
  43.1 0.6 %collective-permute-done.ya = f32[124,128]{1,0:T(8,128)S(1)} collective-permute-done((f32[124,128]{1,0:T(8,128)S(1)}, f32[124,128]{1,0:T(8,128)S(1)}, u32[]{:S(2)}, u32[]{:S(2)}) %collective-permute-start) | collective-permute-done | bytes 63520 | tf_op jit(solution)/shard_map/ppermute | solution.py:354
  43.6 0.0 collective-permute-done.1.yb
  43.7 0.4 base_step.1
  44.0 0.0 collective-permute-done.3.xa
  44.1 0.0 collective-permute-done.2.xb
  44.1 0.0 all-to-all-done
  44.1 1.6 %finish.1 = (f32[3,12,12,128]{3,2,1,0:T(8,128)}, f32[3,6,6,128]{3,2,1,0:T(8,128)}, f32[3,6,6]{2,1,0:T(8,128)}) custom-call(f32[24,512]{1,0:T(8,128)S(1)} %get-tuple-element.18.pick, f32[32,128]{1,0:T(8,128)S(1)} %get-tuple-element.19.rank, f32[32,128]{1,0:T(8,128)S(1)} %get-tuple-element.20.first, f32[32,128]{1,0:T(8,128)S(1)} %get-tuple-element.21.second, ...), custom_call_target="tpu_custom_call" | custom-call | tf_op jit(solution)/shard_map/finish/pallas_call | solution.py:422
  (9 shorter events, 0.0 us)
Async XLA Ops:
  0.6 41.9 %copy-start.8 = (s32[3,4096]{1,0:T(4,128)S(1)}, s32[3,4096]{1,0:T(4,128)}, u32[]{:S(2)}) copy-start(s32[3,4096]{1,0:T(4,128)} %cells.1) | copy-start | bytes 147460
  3.1 21.3 %copy-start = (f32[3,12,12,128]{3,2,1,0:T(8,128)S(1)}, f32[3,12,12,128]{3,2,1,0:T(8,128)}, u32[]{:S(2)}) copy-start(f32[3,12,12,128]{3,2,1,0:T(8,128)} %fine_hbm.1) | copy-start | bytes 663556
  3.2 21.3 %copy-start.1 = (f32[3,6,6,128]{3,2,1,0:T(8,128)S(1)}, f32[3,6,6,128]{3,2,1,0:T(8,128)}, u32[]{:S(2)}) copy-start(f32[3,6,6,128]{3,2,1,0:T(8,128)} %coarse_hbm.1) | copy-start | bytes 165892
  3.2 21.3 %copy-start.2 = (f32[6,6,128]{2,1,0:T(8,128)S(1)}, f32[6,6,128]{2,1,0:T(8,128)}, u32[]{:S(2)}) copy-start(f32[6,6,128]{2,1,0:T(8,128)} %cmu.3) | copy-start | bytes 55300
  3.2 40.5 %copy-start.5 = (f32[3,12,12,128]{3,2,1,0:T(8,128)S(1)}, f32[3,12,12,128]{3,2,1,0:T(8,128)}, u32[]{:S(2)}) copy-start(f32[3,12,12,128]{3,2,1,0:T(8,128)} %prev.1) | copy-start | bytes 663556
  3.2 40.9 %all-to-all-start = ((f32[512,1,128]{2,1,0:T(1,128)}), f32[512,1,128]{2,1,0:T(1,128)S(1)}, u32[]{:S(2)}, u32[]{:S(2)}) async-start(f32[512,1,128]{2,1,0:T(1,128)} %bitcast.5), calls=%async_computation | async-start | bytes 524288 | tf_op jit(solution)/shard_map/all_to_all | solution.py:441
  24.4 19.2 %copy-start.3 = (f32[12,12,128]{2,1,0:T(8,128)S(1)}, f32[12,12,128]{2,1,0:T(8,128)}, u32[]{:S(2)}) copy-start(f32[12,12,128]{2,1,0:T(8,128)} %mu.5) | copy-start | bytes 221188
  24.5 19.2 %copy-start.4 = (f32[12,12,128]{2,1,0:T(8,128)S(1)}, f32[12,12,128]{2,1,0:T(8,128)}, u32[]{:S(2)}) copy-start(f32[12,12,128]{2,1,0:T(8,128)} %coef.3) | copy-start | bytes 221188
  24.5 19.2 %copy-start.7 = (f32[3,6,6,128]{3,2,1,0:T(8,128)S(1)}, f32[3,6,6,128]{3,2,1,0:T(8,128)}, u32[]{:S(2)}) copy-start(f32[3,6,6,128]{3,2,1,0:T(8,128)} %cprev.1) | copy-start | bytes 165892
  24.8 18.8 %collective-permute-start.1 = (f32[136,128]{1,0:T(8,128)S(1)}, f32[136,128]{1,0:T(8,128)S(1)}, u32[]{:S(2)}, u32[]{:S(2)}) collective-permute-start(f32[136,128]{1,0:T(8,128)S(1)} %get-tuple-element.27), channel_id=1, source_target_pairs={{1,2},{3,4},{5,6},{7,8},{9,10},{11,12},{13,14},{2,1},{4,3},{6,5},{... | collective-permute-start | bytes 208904 | tf_op jit(solution)/shard_map/ppermute | solution.py:354
  33.1 10.9 %collective-permute-start.2 = (f32[128,128]{1,0:T(8,128)S(1)}, f32[128,128]{1,0:T(8,128)S(1)}, u32[]{:S(2)}, u32[]{:S(2)}) collective-permute-start(f32[128,128]{1,0:T(8,128)S(1)} %get-tuple-element.31), channel_id=1, source_target_pairs={{16,32},{48,64},{80,96},{112,128},{144,160},{176,192},{208,224},{2... | collective-permute-start | bytes 196616 | tf_op jit(solution)/shard_map/ppermute | solution.py:354
  38.6 5.0 %collective-permute-start = (f32[124,128]{1,0:T(8,128)S(1)}, f32[124,128]{1,0:T(8,128)S(1)}, u32[]{:S(2)}, u32[]{:S(2)}) collective-permute-start(f32[124,128]{1,0:T(8,128)S(1)} %get-tuple-element.26), channel_id=1, source_target_pairs={{0,1},{2,3},{4,5},{6,7},{8,9},{10,11},{12,13},{14,15},{1,0},{3,2},... | collective-permute-start | bytes 190472 | tf_op jit(solution)/shard_map/ppermute | solution.py:354
  40.5 3.1 %copy-start.6 = (f32[6,6,128]{2,1,0:T(8,128)S(1)}, f32[6,6,128]{2,1,0:T(8,128)}, u32[]{:S(2)}) copy-start(f32[6,6,128]{2,1,0:T(8,128)} %ccoef.3) | copy-start | bytes 55300
  40.6 3.5 %collective-permute-start.3 = (f32[120,128]{1,0:T(8,128)S(1)}, f32[120,128]{1,0:T(8,128)S(1)}, u32[]{:S(2)}, u32[]{:S(2)}) collective-permute-start(f32[120,128]{1,0:T(8,128)S(1)} %get-tuple-element.32), channel_id=1, source_target_pairs={{0,16},{32,48},{64,80},{96,112},{128,144},{160,176},{192,208},{224... | collective-permute-start | bytes 184328 | tf_op jit(solution)/shard_map/ppermute | solution.py:354
